TPU v7x, 256 devices: a whole 4x4x8 slice. The times are simulated.
256 devices in a mesh: batch: 8 (over y, x_lo), tm: 32 (over x_hi, z, core).
Axes of the slice: x: 4 (x_hi: 2, x_lo: 2; x = x_hi * 2 + x_lo), y: 4, z: 8, core: 2. Of those that a mesh axis runs over, the one named last changes fastest.
Arguments:
- inputs: bfloat16 [8, 4096, 1536], P('batch', 'tm'), may hold values from -6 to 6
- lengths: int32 [8], P('batch'), may hold values from 2048 to 4096, as said below
- kernel: float32 [31, 1536], replicated, may hold values from -1 to 1
- norm_gain: float32 [1536], replicated, may hold values from 0.25 to 1.75
- weight: bfloat16 [1536, 1536], P('batch'), may hold values from -0.15625 to 0.15625
- cotangent: bfloat16 [8, 4096, 1536], P('batch', 'tm'), may hold values from -6 to 6
Outputs:
- projected: bfloat16 [8, 4096, 1536], P('batch', 'tm')
- grad_input: bfloat16 [8, 4096, 1536], P('batch', 'tm')
- grad_weight: float32 [1536, 1536], P(('batch', 'tm'))
- grad_kernel: float32 [31, 1536], replicated
- grad_gain: float32 [1536], replicated
Inputs may be any that keep to these rules, and one draw needn't show every extreme that they name: `lengths`: some utterance is valid over all 4096 frames.
All inputs are finite; a program needn't handle non-finite values.
Results may differ from a plain program's by a relative error of at most 0.0049.
Values may be sent and summed in bfloat16 or wider, within the bound.
A program may use at most 64 MiB of HBM per device.

v0:
```python
import jax
import jax.numpy as jnp
from jax import lax
from jax.experimental import pallas as pl
from jax.experimental.pallas import tpu as pltpu
from jax.sharding import PartitionSpec as P

F32, BF16 = jnp.float32, jnp.bfloat16
MESH = pl.DeviceIdType.MESH
D, T, H, TAPS = 1536, 128, 768, 31
PAD = 16
CX, CY = 256, 512
LANES = 128
CHUNKS = D // LANES


def lanes_of(k):
    return pl.ds(pl.multiple_of(k * LANES, LANES), LANES)


def fused(
    x_hbm, len_hbm, kern_hbm, gain_hbm, w_hbm, cot_hbm,
    proj_hbm, gin_hbm, gw_hbm, gk_hbm, gg_hbm,
    len_ref, x_ref, kern_ref, gain_ref, cot_ref, proj_ref, gin_ref, gw_ref, gk_ref, gg_ref,
    xm, hx, xf, cv, ds, rs_sum, ab, tf, tp, at2, atm, us, ub, wb, px, py, rx, ry, s2x, s2y, r2x, r2y,
    facc, zs, rz, fin, cr, agp, agr, pj, pjr, cg, gkb, gcr, gh, zr, xs, ys, fg, fgr,
    sem_halo_s, sem_halo_r, sem_w_s, sem_w_r, sem_c_s, sem_c_r, sem_p_s, sem_p_r,
    sem_z_s, sem_z_r, sem_t_s, sem_t_r, sem_a_s, sem_a_r, sem_in, sem_out,
):
    b = lax.axis_index("batch")
    t = lax.axis_index("tm")
    y, xl = b // 2, b % 2
    xh, z, c = t // 16, (t // 2) % 8, t % 2
    x = xh * 2 + xl
    oc = 1 - c

    def dev(y_, x_, z_, c_):
        return (y_ * 2 + x_ % 2, (x_ // 2) * 16 + z_ * 2 + c_)

    def along_y(i):
        return dev((y + i) % 4, x, z, c)

    def along_x(i):
        return dev(y, (x + i) % 4, z, c)

    def along_z(i):
        return dev(y, x, (z + i) % 8, c)

    mate = dev(y, x, z, oc)
    zp = z % 2
    z_mate = z + 1 - 2 * zp
    across, diagonal = dev(y, x, z_mate, c), dev(y, x, z_mate, oc)
    before, after = (b, t - 1), (b, t + 1)

    def block_of(x_):
        return (x_ % 2) * 2 + x_ // 2

    q = block_of(x)

    def half(c_):
        return pl.ds(pl.multiple_of(c_ * H, H), H)

    def frames_of(c_):
        return pl.ds(pl.multiple_of(c_ * T, T), T)

    started = []

    def copy(src, dst, ss, rs, to):
        return pltpu.make_async_remote_copy(
            src_ref=src, dst_ref=dst, send_sem=ss, recv_sem=rs, device_id=to, device_id_type=MESH
        )

    def send(*args):
        item = copy(*args)
        item.start()
        started.append(item)
        return item

    barrier = pltpu.get_barrier_semaphore()

    def greet(to):
        pl.semaphore_signal(barrier, inc=1, device_id=to, device_id_type=MESH)

    greet(mate)
    greet(diagonal)
    for i in range(1, 4):
        greet(along_y(i))
        greet(along_x(i))
    for i in range(1, 8):
        greet(along_z(i))

    @pl.when(t > 0)
    def _():
        greet(before)

    @pl.when(t < 31)
    def _():
        greet(after)

    w_own = pl.ds(pl.multiple_of((y * 2 + xl) * 192, 192), 192)
    loads = [
        pltpu.make_async_copy(src, dst, sem_in.at[n])
        for n, (src, dst) in enumerate((
            (x_hbm, x_ref), (cot_hbm, cot_ref), (w_hbm.at[:, half(c)], wb.at[w_own]),
            (kern_hbm, kern_ref), (gain_hbm, gain_ref), (len_hbm, len_ref),
        ))
    ]
    for item in loads:
        item.start()
    loads[5].wait()
    position = t * T + lax.broadcasted_iota(jnp.int32, (T, LANES), 0)
    live = jnp.where(position < len_ref[0], 1.0, 0.0).astype(F32)
    for item in loads[:2]:
        item.wait()

    def mask_chunk(k, _):
        at_lanes = lanes_of(k)
        masked = x_ref[:, at_lanes].astype(F32) * live
        xm[:, at_lanes] = masked.astype(BF16)
        xf[PAD:PAD + T, at_lanes] = masked
        us[:, at_lanes] = (cot_ref[:, at_lanes].astype(F32) * live).astype(BF16)
        return 0

    lax.fori_loop(0, CHUNKS, mask_chunk, 0)

    others = 15 + jnp.where(t > 0, 1, 0) + jnp.where(t < 31, 1, 0)
    pl.semaphore_wait(barrier, others)

    to_before = copy(xm.at[pl.ds(0, PAD)], hx.at[1], sem_halo_s.at[0], sem_halo_r.at[1], before)
    to_after = copy(xm.at[pl.ds(T - PAD, PAD)], hx.at[0], sem_halo_s.at[1], sem_halo_r.at[0], after)

    @pl.when(t > 0)
    def _():
        to_before.start()

    @pl.when(t < 31)
    def _():
        to_after.start()

    mine = zp * 2 + c
    u_swaps = [send(us.at[:, half(oc)], ub.at[frames_of(mine)], sem_c_s.at[0], sem_c_r.at[0], mate)]

    def rows_of(y_, xl_, side):
        return wb.at[pl.ds(pl.multiple_of((y_ * 2 + xl_) * 192 + side * 96, 96), 96)]

    y_up, y_down, y_far = (y + 1) % 4, (y + 3) % 4, (y + 2) % 4
    x_step = (1, 3)

    def push(here, n, to):
        send(here, here, sem_w_s.at[n], sem_w_r.at[n], to)

    def landed(here, n):
        copy(here, here, sem_w_s.at[n], sem_w_r.at[n], mate).wait_recv()

    loads[2].wait()
    for side in range(2):
        own = rows_of(y, xl, side)
        push(own, side, along_y(1))
        push(own, 2 + side, along_y(3))
        push(own, 6 + side, along_x(x_step[side]))
    u_swaps += [
        send(us.at[:, half(c_)], ub.at[frames_of(mine)], sem_a_s.at[n], sem_a_r.at[n], to)
        for n, c_, to in ((0, c, across), (1, oc, diagonal))
    ]
    ub[frames_of(mine), :] = us[:, half(c)]

    for item in loads[3:5]:
        item.wait()

    def conv(source, taps, forward):
        count = source.shape[0] - 32
        total = jnp.zeros((count, LANES), F32)
        for r in range(8):
            shifted = source[r:r + count + 24]
            for k in range(4):
                offset = 8 * k + r
                tap = offset - 1 if forward else TAPS - offset
                if 0 <= tap < TAPS:
                    total = total + taps[tap:tap + 1] * shifted[8 * k:8 * k + count]
        return total

    def conv_chunk(start, count):
        def body(k, total):
            at_lanes = lanes_of(k)
            value = conv(xf[start:start + count + 32, at_lanes], kern_ref[:, at_lanes], True)
            value = value * live[start:start + count]
            cv[start:start + count, at_lanes] = value
            return total + value
        rs_sum[start:start + count, :] = lax.fori_loop(0, CHUNKS, body, jnp.zeros((count, LANES), F32))

    conv_chunk(PAD, T - 2 * PAD)

    @pl.when(t > 0)
    def _():
        to_after.wait_recv()
        xf[0:PAD, :] = hx[0].astype(F32)

    @pl.when(t == 0)
    def _():
        xf[0:PAD, :] = jnp.zeros((PAD, D), F32)

    @pl.when(t < 31)
    def _():
        to_before.wait_recv()
        xf[PAD + T:, :] = hx[1].astype(F32)

    @pl.when(t == 31)
    def _():
        xf[PAD + T:, :] = jnp.zeros((PAD, D), F32)

    conv_chunk(0, PAD)
    conv_chunk(T - PAD, PAD)

    zero = jnp.zeros((T, LANES), F32)
    total = rs_sum[...]
    average = jnp.broadcast_to(jnp.sum(total, axis=1, keepdims=True) * (1.0 / D), (T, LANES))

    def variance_chunk(k, total):
        centred = cv[:, lanes_of(k)] - average
        return total + centred * centred

    total = lax.fori_loop(0, CHUNKS, variance_chunk, zero)
    variance = jnp.sum(total, axis=1, keepdims=True) * (1.0 / D)
    inv = jnp.broadcast_to(lax.rsqrt(variance + 1e-05), (T, LANES))

    def act_chunk(k, _):
        at_lanes = lanes_of(k)
        normed = (cv[:, at_lanes] - average) * inv
        scaled = normed * gain_ref[at_lanes][None]
        gate = 1.0 / (1.0 + jnp.exp(-scaled))
        act = scaled * gate
        cv[:, at_lanes] = normed
        ds[:, at_lanes] = gate * (1.0 + scaled * (1.0 - gate))
        ab[frames_of(c), at_lanes] = act.astype(BF16)
        tf[pl.ds(pl.multiple_of((k % 3) * LANES, LANES), LANES), :] = act.T
        return 0

    swaps, z_swaps, a_swaps = [], [], []
    for part in range(4):
        lax.fori_loop(part * 3, part * 3 + 3, act_chunk, 0)
        for parity in range(2):
            for g in range(16):
                tp[12 * g:12 * g + 12, :] = tf[24 * g + 12 * parity:24 * g + 12 * parity + 12, :]
            at2[parity, part * 192:part * 192 + 192, :] = tp[...].astype(BF16)
        rows = pl.ds(part * 192, 192)
        there = atm.at[rows, frames_of(mine)]
        z_swaps.append(send(at2.at[1 - zp, rows], there, sem_a_s.at[2 + part], sem_a_r.at[2 + part], across))
        swaps.append(send(at2.at[zp, rows], there, sem_c_s.at[1 + part], sem_c_r.at[1 + part], mate))
        atm[rows, frames_of(mine)] = at2[zp, part * 192:part * 192 + 192, :]
    here = ab.at[frames_of(c)]
    a_swaps.append(send(here, here, sem_c_s.at[5], sem_c_r.at[5], mate))

    for side in range(2):
        for n, from_y in ((0, y_down), (2, y_up)):
            here = rows_of(from_y, xl, side)
            landed(here, n + side)
            push(here, 8 + n + side, along_x(x_step[side]))
            if n == 0 and side == 0:
                push(here, 4, along_y(1))
            if n == 2 and side == 1:
                push(here, 5, along_y(3))

    theirs = (1 - zp) * 2 + c
    for part in range(4):
        z_swaps[part].wait_recv()
        here = atm.at[pl.ds(part * 192, 192), frames_of(theirs)]
        swaps.append(send(here, here, sem_a_s.at[6 + part], sem_a_r.at[6 + part], mate))

    for side in range(2):
        here = rows_of(y_far, xl, side)
        landed(here, 4 + side)
        push(here, 12 + side, along_x(x_step[side]))

    for item in u_swaps + swaps:
        item.wait_recv()

    def partial(n, start, width):
        rows = pl.ds(pl.multiple_of(n * 192, 192), 192)
        value = jnp.dot(atm[rows, :], ub[:, start:start + width], preferred_element_type=F32)
        return value.reshape(4, 48, width).astype(BF16)

    y_first = []
    for i in (1, 3, 2, 0):
        to_y = (y + i) % 4
        py[to_y] = partial(to_y, CX, CY)
        if i:
            y_first.append(send(py.at[to_y], ry.at[i - 1], sem_p_s.at[2 + i], sem_p_r.at[2 + i], along_y(i)))

    def partial_x(n, _):
        px[n] = partial(n, 0, CX)
        return 0

    lax.fori_loop(0, 4, partial_x, 0)
    x_first = [
        send(px.at[:, block_of((x + i) % 4)], rx.at[i - 1], sem_p_s.at[i - 1], sem_p_r.at[i - 1], along_x(i))
        for i in (1, 3, 2)
    ]

    ag_swaps = []
    chip_rows = pl.ds(pl.multiple_of(zp * 2 * T, 2 * T), 2 * T)
    for n, from_y in ((6, y), (8, y_down), (10, y_up), (12, y_far)):
        for side in range(2):
            landed(rows_of(from_y, 1 - xl, side), n + side)
        cols = pl.ds(pl.multiple_of(from_y * 384, 384), 384)
        value = lax.dot_general(
            ub[chip_rows, :], wb[cols, :], (((1,), (1,)), ((), ())), preferred_element_type=F32
        )
        agp[0, :, cols] = value[:T]
        agp[1, :, cols] = value[T:]
        k = len(ag_swaps)
        ag_swaps.append(
            send(agp.at[oc, :, cols], agr.at[:, cols], sem_c_s.at[6 + k], sem_c_r.at[6 + k], mate)
        )

    for item in a_swaps:
        item.wait_recv()

    def project_chunk(n, _):
        cols = pl.ds(pl.multiple_of(n * 256, 256), 256)
        value = jnp.dot(ab[...], wb[:, cols], preferred_element_type=F32).astype(BF16)
        pj[0, :, cols] = value[:T]
        pj[1, :, cols] = value[T:]
        return 0

    lax.fori_loop(0, 3, project_chunk, 0)
    pj_swap = send(pj.at[oc], pjr, sem_c_s.at[10], sem_c_r.at[10], mate)
    proj_ref[:, half(c)] = pj[c]

    for item in ag_swaps:
        item.wait_recv()

    def back_chunk(k, sums):
        at_lanes = lanes_of(k)
        normed = cv[:, at_lanes]
        scaled_grad = (agp[c, :, at_lanes] + agr[:, at_lanes]) * ds[:, at_lanes]
        gkb[TAPS:TAPS + 1, at_lanes] = jnp.sum(scaled_grad * normed, axis=0, keepdims=True)
        normed_grad = scaled_grad * gain_ref[at_lanes][None]
        ds[:, at_lanes] = normed_grad
        return (sums[0] + normed_grad, sums[1] + normed_grad * normed)

    sums = lax.fori_loop(0, CHUNKS, back_chunk, (zero, zero))
    first, second = [
        jnp.broadcast_to(jnp.sum(s, axis=1, keepdims=True) * (1.0 / D), (T, LANES)) for s in sums
    ]
    inv_live = inv * live

    def conv_grad_chunk(k, _):
        at_lanes = lanes_of(k)
        cg[PAD:PAD + T, at_lanes] = inv_live * (ds[:, at_lanes] - first - cv[:, at_lanes] * second)
        return 0

    lax.fori_loop(0, CHUNKS, conv_grad_chunk, 0)

    g_before = copy(cg.at[pl.ds(PAD, PAD)], cg.at[pl.ds(PAD + T, PAD)], sem_halo_s.at[2], sem_halo_r.at[3], before)
    g_after = copy(cg.at[pl.ds(T, PAD)], cg.at[pl.ds(0, PAD)], sem_halo_s.at[3], sem_halo_r.at[2], after)

    @pl.when(t > 0)
    def _():
        g_before.start()

    @pl.when(t < 31)
    def _():
        g_after.start()

    def taps_chunk(k, _):
        at_lanes = lanes_of(k)
        source = xf[:, at_lanes]
        grad = cg[PAD:PAD + T, at_lanes]
        for r in range(8):
            shifted = source[r:r + T + 24]
            for j in range(4):
                tap = 8 * j + r - 1
                if 0 <= tap < TAPS:
                    gkb[tap:tap + 1, at_lanes] = jnp.sum(grad * shifted[8 * j:8 * j + T], axis=0, keepdims=True)
        return 0

    lax.fori_loop(oc * 6, oc * 6 + 6, taps_chunk, 0)
    gk_swap = send(gkb.at[:, half(oc)], gcr, sem_t_s.at[0], sem_t_r.at[0], mate)
    lax.fori_loop(c * 6, c * 6 + 6, taps_chunk, 0)

    def piece(z_):
        return (
            pl.ds(pl.multiple_of((z_ // 2) * 8, 8), 8),
            pl.ds(pl.multiple_of((z_ % 2) * 384, 384), 384),
        )

    gk_swap.wait_recv()
    gh[...] = gkb[:, half(c)] + gcr[...]
    t_z = [
        send(gh.at[piece((z + i) % 8)], zr.at[i - 1], sem_t_s.at[i], sem_t_r.at[i], along_z(i))
        for i in (4, 3, 5, 2, 6, 1, 7)
    ]

    def add(first, own, came, out):
        for item in first:
            item.wait_recv()

        def body(n, _):
            value = own(n).astype(F32)
            for i in range(3):
                value = value + came[i, n].astype(F32)
            out[n] = value.astype(BF16)
            return 0

        lax.fori_loop(0, 4, body, 0)

    add(x_first, lambda n: px[n, q], rx, s2x)
    x_second = [
        send(s2x.at[(y + i) % 4], r2x.at[i - 1], sem_p_s.at[5 + i], sem_p_r.at[5 + i], along_y(i))
        for i in (2, 1, 3)
    ]
    add(y_first, lambda n: py[y, n], ry, s2y)
    y_second = [
        send(s2y.at[block_of((x + i) % 4)], r2y.at[i - 1], sem_p_s.at[8 + i], sem_p_r.at[8 + i], along_x(i))
        for i in (2, 1, 3)
    ]

    @pl.when(t > 0)
    def _():
        g_after.wait_recv()

    @pl.when(t == 0)
    def _():
        cg[0:PAD, :] = jnp.zeros((PAD, D), F32)

    @pl.when(t < 31)
    def _():
        g_before.wait_recv()

    @pl.when(t == 31)
    def _():
        cg[PAD + T:, :] = jnp.zeros((PAD, D), F32)

    def input_chunk(k, _):
        at_lanes = lanes_of(k)
        value = conv(cg[:, at_lanes], kern_ref[:, at_lanes], False) * live
        gin_ref[:, at_lanes] = value.astype(BF16)
        return 0

    lax.fori_loop(0, 6, input_chunk, 0)

    for item in t_z:
        item.wait_recv()
    mine_t = gh[piece(z)]
    for i in range(7):
        mine_t = mine_t + zr[i]
    xs[x] = mine_t
    for i in (2, 1, 3):
        send(xs.at[x], xs.at[x], sem_t_s.at[7 + i], sem_t_r.at[7 + i], along_x(i))

    def wait_slots(slots, me, base):
        for i in range(1, 4):
            slot = slots.at[(me + 4 - i) % 4]
            copy(slot, slot, sem_t_s.at[base + i], sem_t_r.at[base + i], mate).wait_recv()

    for item in x_second + y_second:
        item.wait_recv()
    left, right = s2x[y].astype(F32), s2y[q].astype(F32)
    for i in range(3):
        left = left + r2x[i].astype(F32)
        right = right + r2y[i].astype(F32)
    facc[0:48, 0:CX] = left
    facc[0:48, CX:H] = right
    facc[48:56, :] = jnp.zeros((8, H), F32)
    for n in range(4):
        zs[n] = facc[12 * n:12 * n + 16, :].astype(BF16)
    w_z = [
        send(zs.at[(z // 2 + i) % 4], rz.at[i - 1], sem_z_s.at[i - 1], sem_z_r.at[i - 1], along_z(2 * i))
        for i in (2, 1, 3)
    ]

    wait_slots(xs, x, 7)
    ys[y] = xs[0] + xs[1] + xs[2] + xs[3]
    for i in (2, 1, 3):
        send(ys.at[y], ys.at[y], sem_t_s.at[10 + i], sem_t_r.at[10 + i], along_y(i))
    lax.fori_loop(6, CHUNKS, input_chunk, 0)
    wait_slots(ys, y, 10)
    fg[piece(z)] = ys[0] + ys[1] + ys[2] + ys[3]
    for i in (4, 3, 5, 2, 6, 1, 7):
        here = fg.at[piece(z)]
        send(here, here, sem_t_s.at[13 + i], sem_t_r.at[13 + i], along_z(i))

    stores = [pltpu.make_async_copy(gin_ref, gin_hbm, sem_out.at[0])]
    stores[0].start()
    pj_swap.wait_recv()
    proj_ref[:, half(oc)] = pjr[...]
    stores.append(pltpu.make_async_copy(proj_ref, proj_hbm, sem_out.at[1]))
    stores[1].start()

    for item in w_z:
        item.wait_recv()
    rows = zs[z // 2].astype(F32)
    for i in range(3):
        rows = rows + rz[i].astype(F32)
    fin[...] = jnp.zeros((2, 8, H), F32)
    fin[0, 0:6, :] = rows[0:6]
    fin[1, 0:6, :] = rows[6:12]
    w_swap = send(fin.at[oc], cr, sem_z_s.at[3], sem_z_r.at[3], mate)

    for i in range(1, 8):
        slot = fg.at[piece((z + 8 - i) % 8)]
        copy(slot, slot, sem_t_s.at[13 + i], sem_t_r.at[13 + i], mate).wait_recv()
    t_swap = send(fg, fgr, sem_t_s.at[21], sem_t_r.at[21], mate)

    def put_taps(cols, value):
        gk_ref[:, cols] = value[0:TAPS]
        gg_ref[:, cols] = value[TAPS:TAPS + 1]

    put_taps(half(c), fg[...])
    gw_ref[:, half(c)] = fin[c][0:6]
    t_swap.wait_recv()
    put_taps(half(oc), fgr[...])
    w_swap.wait_recv()
    gw_ref[:, half(oc)] = cr[0:6, :]
    for n, (src, dst) in enumerate(((gw_ref, gw_hbm), (gk_ref, gk_hbm), (gg_ref, gg_hbm))):
        stores.append(pltpu.make_async_copy(src, dst, sem_out.at[2 + n]))
        stores[-1].start()

    @pl.when(t > 0)
    def _():
        to_before.wait_send()
        g_before.wait_send()

    @pl.when(t < 31)
    def _():
        to_after.wait_send()
        g_after.wait_send()

    for item in started:
        item.wait_send()
    for item in stores:
        item.wait()


def deliver(*refs):
    sources, results, kept, sems = refs[:5], refs[5:10], refs[10:15], refs[15]
    loads = [pltpu.make_async_copy(a, b, sems.at[n]) for n, (a, b) in enumerate(zip(sources, kept))]
    stores = [pltpu.make_async_copy(a, b, sems.at[5 + n]) for n, (a, b) in enumerate(zip(kept, results))]
    for item in loads:
        item.start()
    for first, then in zip(loads, stores):
        first.wait()
        then.start()
    for item in stores:
        item.wait()


def on_device(inputs, lengths, kernel, norm_gain, weight, cotangent):
    vmem = pl.BlockSpec(memory_space=pltpu.VMEM)
    dma = pltpu.SemaphoreType.DMA
    scratch = [
        pltpu.SMEM((1,), jnp.int32),
        pltpu.VMEM((T, D), BF16),
        pltpu.VMEM((TAPS, D), F32),
        pltpu.VMEM((D,), F32),
        pltpu.VMEM((T, D), BF16),
        pltpu.VMEM((T, D), BF16),
        pltpu.VMEM((T, D), BF16),
        pltpu.VMEM((6, D), F32),
        pltpu.VMEM((TAPS, D), F32),
        pltpu.VMEM((1, D), F32),
        pltpu.VMEM((T, D), BF16),
        pltpu.VMEM((2, PAD, D), BF16),
        pltpu.VMEM((T + 2 * PAD, D), F32),
        pltpu.VMEM((T, D), F32),
        pltpu.VMEM((T, D), F32),
        pltpu.VMEM((T, LANES), F32),
        pltpu.VMEM((2 * T, D), BF16),
        pltpu.VMEM((3 * LANES, T), F32),
        pltpu.VMEM((192, T), F32),
        pltpu.VMEM((2, H, T), BF16),
        pltpu.VMEM((H, 4 * T), BF16),
        pltpu.VMEM((T, D), BF16),
        pltpu.VMEM((4 * T, H), BF16),
        pltpu.VMEM((D, H), BF16),
        pltpu.VMEM((4, 4, 48, CX), BF16),
        pltpu.VMEM((4, 4, 48, CY), BF16),
        pltpu.VMEM((3, 4, 48, CX), BF16),
        pltpu.VMEM((3, 4, 48, CY), BF16),
        pltpu.VMEM((4, 48, CX), BF16),
        pltpu.VMEM((4, 48, CY), BF16),
        pltpu.VMEM((3, 48, CX), BF16),
        pltpu.VMEM((3, 48, CY), BF16),
        pltpu.VMEM((56, H), F32),
        pltpu.VMEM((4, 16, H), BF16),
        pltpu.VMEM((3, 16, H), BF16),
        pltpu.VMEM((2, 8, H), F32),
        pltpu.VMEM((8, H), F32),
        pltpu.VMEM((2, T, D), F32),
        pltpu.VMEM((T, D), F32),
        pltpu.VMEM((2, T, H), BF16),
        pltpu.VMEM((T, H), BF16),
        pltpu.VMEM((T + 2 * PAD, D), F32),
        pltpu.VMEM((32, D), F32),
        pltpu.VMEM((32, H), F32),
        pltpu.VMEM((32, H), F32),
        pltpu.VMEM((7, 8, 384), F32),
        pltpu.VMEM((4, 8, 384), F32),
        pltpu.VMEM((4, 8, 384), F32),
        pltpu.VMEM((32, H), F32),
        pltpu.VMEM((32, H), F32),
        dma((4,)), dma((4,)),
        dma((14,)), dma((14,)),
        dma((12,)), dma((12,)),
        dma((12,)), dma((12,)),
        dma((8,)), dma((8,)),
        dma((22,)), dma((22,)),
        dma((10,)), dma((10,)),
        dma((6,)), dma((5,)),
    ]
    hbm = pl.BlockSpec(memory_space=pl.ANY)
    shapes = (
        jax.ShapeDtypeStruct((T, D), BF16),
        jax.ShapeDtypeStruct((T, D), BF16),
        jax.ShapeDtypeStruct((6, D), F32),
        jax.ShapeDtypeStruct((TAPS, D), F32),
        jax.ShapeDtypeStruct((1, D), F32),
    )
    results = pl.pallas_call(
        fused,
        out_shape=shapes,
        in_specs=[hbm] * 6,
        out_specs=[hbm] * 5,
        scratch_shapes=scratch,
        compiler_params=pltpu.CompilerParams(
            collective_id=0, has_side_effects=True, vmem_limit_bytes=60 << 20
        ),
        name="conv_module",
    )(inputs[0], lengths, kernel, norm_gain, weight, cotangent[0])
    projected, grad_input, grad_weight, grad_kernel, grad_gain = pl.pallas_call(
        deliver,
        out_shape=shapes,
        in_specs=[hbm] * 5,
        out_specs=[hbm] * 5,
        scratch_shapes=[pltpu.VMEM(r.shape, r.dtype) for r in shapes] + [dma((10,))],
        compiler_params=pltpu.CompilerParams(vmem_limit_bytes=60 << 20),
        name="deliver",
    )(*results)
    return (projected[None], grad_input[None], grad_weight, grad_kernel, grad_gain[0])


def solution(mesh):
    in_specs = (
        P("batch", "tm", None),
        P("batch"),
        P(),
        P(),
        P("batch", None),
        P("batch", "tm", None),
    )
    out_specs = (P("batch", "tm", None), P("batch", "tm", None), P(("batch", "tm"), None), P(), P())
    return jax.shard_map(
        on_device, mesh=mesh, in_specs=in_specs, out_specs=out_specs, check_vma=False
    )
```

profile of v0, /device:TPU:1, one launch (start us, length us, event | category | flops | bytes accessed | tf_op | source)
XLA Modules:
  0.0 60.5 jit_solution(7038995165993039145)
XLA Ops:
  1.3 55.9 %conv_module.1 = (bf16[128,1536]{1,0:T(8,128)(2,1)}, bf16[128,1536]{1,0:T(8,128)(2,1)}, f32[6,1536]{1,0:T(8,128)}, f32[31,1536]{1,0:T(8,128)}, f32[1,1536]{1,0:T(1,128)}) custom-call(bf16[128,1536]{1,0:T(8,128)(2,1)} %bitcast.4, s32[1]{0:T(128)S(6)} %copy.11.len_hbm, f32[31,1536]{1,0:T(8,128)} %kern_hbm.1, f32[1536]{0:T(1024)} %gain_hbm.1, ...), custom_call_target="tpu_custom_call" | custom-call | tf_op jit(solution)/shard_map/conv_module/pallas_call | solution.py:619
  57.2 2.0 %deliver.1 = (bf16[128,1536]{1,0:T(8,128)(2,1)}, bf16[128,1536]{1,0:T(8,128)(2,1)}, f32[6,1536]{1,0:T(8,128)}, f32[31,1536]{1,0:T(8,128)}, f32[1,1536]{1,0:T(1,128)}) custom-call(bf16[128,1536]{1,0:T(8,128)(2,1)} %get-tuple-element.15.refs_0_, bf16[128,1536]{1,0:T(8,128)(2,1)} %get-tuple-element.16.refs_1_, f32[6,1536]{1,0:T(8,128)} %get-tuple-element.17.refs_2_, ...), custom_call_target="tpu_custom_call" | custom-call | tf_op jit(solution)/shard_map/deliver/pallas_call | solution.py:630
  59.2 0.0 copy-start
  59.2 0.7 %copy-done = f32[1,1536]{1,0:T(1,128)S(1)} copy-done((f32[1,1536]{1,0:T(1,128)S(1)}, f32[1,1536]{1,0:T(1,128)}, u32[]{:S(2)}) %copy-start) | copy-done | bytes 6168
  59.9 0.6 %reduce = f32[1536]{0:T(1024)} reduce(f32[1,1536]{1,0:T(1,128)S(1)} %copy-done, f32[]{:T(128)} %constant.3), dimensions={0}, to_apply=%get-tuple-element.24.reduce_sub_computation | reduce | bytes 12292 | tf_op jit(solution)/shard_map/deliver/pallas_call | solution.py:630
Async XLA Ops:
  59.2 0.7 %copy-start = (f32[1,1536]{1,0:T(1,128)S(1)}, f32[1,1536]{1,0:T(1,128)}, u32[]{:S(2)}) copy-start(f32[1,1536]{1,0:T(1,128)} %get-tuple-element.24) | copy-start | bytes 18436
where the time goes:
time: 60.7 us; the launch traced here: 60.5 us
  Pallas kernels  57.9 us (95%)
  between operations  1.3 us (2%)
  local copies, waits for them, and re-layouts  0.69 us (1%)
  other arithmetic  0.62 us (1%)
    pallas_call x1, Pallas kernels, on_device(): pl.pallas_call(fused, out_shape=shapes, in_specs=[hbm] * 6, out_specs=[hb...  55.9 us
    pallas_call x1, Pallas kernels, on_device(): pl.pallas_call(deliver, out_shape=shapes, in_specs=[hbm] * 5, out_specs=[...  2.04 us

commit v1 on v0

--- a/solution.py
+++ b/solution.py
@@ -9,7 +9,7 @@
 MESH = pl.DeviceIdType.MESH
 D, T, H, TAPS = 1536, 128, 768, 31
 PAD = 16
-CX, CY = 256, 512
+CX, CY = 384, 384
 LANES = 128
 CHUNKS = D // LANES
 
@@ -23,7 +23,7 @@
     proj_hbm, gin_hbm, gw_hbm, gk_hbm, gg_hbm,
     len_ref, x_ref, kern_ref, gain_ref, cot_ref, proj_ref, gin_ref, gw_ref, gk_ref, gg_ref,
     xm, hx, xf, cv, ds, rs_sum, ab, tf, tp, at2, atm, us, ub, wb, px, py, rx, ry, s2x, s2y, r2x, r2y,
-    facc, zs, rz, fin, cr, agp, agr, pj, pjr, cg, gkb, gcr, gh, zr, xs, ys, fg, fgr,
+    facc, zs, rz, fin, cr, agp, agr, pj, pjr, cg, gkb, gcr, gh, zr, xs, fg, fgr,
     sem_halo_s, sem_halo_r, sem_w_s, sem_w_r, sem_c_s, sem_c_r, sem_p_s, sem_p_r,
     sem_z_s, sem_z_r, sem_t_s, sem_t_r, sem_a_s, sem_a_r, sem_in, sem_out,
 ):
@@ -83,9 +83,8 @@
 
     greet(mate)
     greet(diagonal)
-    for i in range(1, 4):
-        greet(along_y(i))
-        greet(along_x(i))
+    for i in range(1, 16):
+        greet(dev((y + i // 4) % 4, (x + i % 4) % 4, z, c))
     for i in range(1, 8):
         greet(along_z(i))
 
@@ -107,6 +106,31 @@
     ]
     for item in loads:
         item.start()
+    others = 24 + jnp.where(t > 0, 1, 0) + jnp.where(t < 31, 1, 0)
+    pl.semaphore_wait(barrier, others)
+
+    def rows_of(y_, xl_, side):
+        return wb.at[pl.ds(pl.multiple_of((y_ * 2 + xl_) * 192 + side * 96, 96), 96)]
+
+    y_up, y_down, y_far = (y + 1) % 4, (y + 3) % 4, (y + 2) % 4
+    x_step = (1, 3)
+
+    def push(here, n, to):
+        send(here, here, sem_w_s.at[n], sem_w_r.at[n], to)
+
+    def landed(here, n):
+        copy(here, here, sem_w_s.at[n], sem_w_r.at[n], mate).wait_recv()
+
+    def push_own(side, n, to):
+        send(w_hbm.at[pl.ds(side * 96, 96), half(c)], rows_of(y, xl, side), sem_w_s.at[n], sem_w_r.at[n], to)
+
+    push_own(0, 0, along_y(1))
+    push_own(1, 3, along_y(3))
+    for side in range(2):
+        push_own(side, 6 + side, along_x(x_step[side]))
+    push_own(1, 1, along_y(1))
+    push_own(0, 2, along_y(3))
+
     loads[5].wait()
     position = t * T + lax.broadcasted_iota(jnp.int32, (T, LANES), 0)
     live = jnp.where(position < len_ref[0], 1.0, 0.0).astype(F32)
@@ -123,9 +147,6 @@
 
     lax.fori_loop(0, CHUNKS, mask_chunk, 0)
 
-    others = 15 + jnp.where(t > 0, 1, 0) + jnp.where(t < 31, 1, 0)
-    pl.semaphore_wait(barrier, others)
-
     to_before = copy(xm.at[pl.ds(0, PAD)], hx.at[1], sem_halo_s.at[0], sem_halo_r.at[1], before)
     to_after = copy(xm.at[pl.ds(T - PAD, PAD)], hx.at[0], sem_halo_s.at[1], sem_halo_r.at[0], after)
 
@@ -140,24 +161,6 @@
     mine = zp * 2 + c
     u_swaps = [send(us.at[:, half(oc)], ub.at[frames_of(mine)], sem_c_s.at[0], sem_c_r.at[0], mate)]
 
-    def rows_of(y_, xl_, side):
-        return wb.at[pl.ds(pl.multiple_of((y_ * 2 + xl_) * 192 + side * 96, 96), 96)]
-
-    y_up, y_down, y_far = (y + 1) % 4, (y + 3) % 4, (y + 2) % 4
-    x_step = (1, 3)
-
-    def push(here, n, to):
-        send(here, here, sem_w_s.at[n], sem_w_r.at[n], to)
-
-    def landed(here, n):
-        copy(here, here, sem_w_s.at[n], sem_w_r.at[n], mate).wait_recv()
-
-    loads[2].wait()
-    for side in range(2):
-        own = rows_of(y, xl, side)
-        push(own, side, along_y(1))
-        push(own, 2 + side, along_y(3))
-        push(own, 6 + side, along_x(x_step[side]))
     u_swaps += [
         send(us.at[:, half(c_)], ub.at[frames_of(mine)], sem_a_s.at[n], sem_a_r.at[n], to)
         for n, c_, to in ((0, c, across), (1, oc, diagonal))
@@ -169,14 +172,17 @@
 
     def conv(source, taps, forward):
         count = source.shape[0] - 32
-        total = jnp.zeros((count, LANES), F32)
+        total = None
         for r in range(8):
-            shifted = source[r:r + count + 24]
+            part = None
             for k in range(4):
                 offset = 8 * k + r
                 tap = offset - 1 if forward else TAPS - offset
                 if 0 <= tap < TAPS:
-                    total = total + taps[tap:tap + 1] * shifted[8 * k:8 * k + count]
+                    value = taps[tap:tap + 1] * source[8 * k:8 * k + count + 8]
+                    part = value if part is None else part + value
+            part = part[r:r + count]
+            total = part if total is None else total + part
         return total
 
     def conv_chunk(start, count):
@@ -234,6 +240,16 @@
         ab[frames_of(c), at_lanes] = act.astype(BF16)
         tf[pl.ds(pl.multiple_of((k % 3) * LANES, LANES), LANES), :] = act.T
         return 0
+
+    def pass_on(*pieces):
+        for n, from_y, side in pieces:
+            here = rows_of(from_y, xl, side)
+            landed(here, n + side)
+            push(here, 8 + n + side, along_x(x_step[side]))
+
+    pass_on((0, y_down, 0), (2, y_up, 1))
+    push(rows_of(y_down, xl, 0), 4, along_y(1))
+    push(rows_of(y_up, xl, 1), 5, along_y(3))
 
     swaps, z_swaps, a_swaps = [], [], []
     for part in range(4):
@@ -250,15 +266,11 @@
     here = ab.at[frames_of(c)]
     a_swaps.append(send(here, here, sem_c_s.at[5], sem_c_r.at[5], mate))
 
+    pass_on((2, y_up, 0), (0, y_down, 1))
     for side in range(2):
-        for n, from_y in ((0, y_down), (2, y_up)):
-            here = rows_of(from_y, xl, side)
-            landed(here, n + side)
-            push(here, 8 + n + side, along_x(x_step[side]))
-            if n == 0 and side == 0:
-                push(here, 4, along_y(1))
-            if n == 2 and side == 1:
-                push(here, 5, along_y(3))
+        here = rows_of(y_far, xl, side)
+        landed(here, 4 + side)
+        push(here, 12 + side, along_x(x_step[side]))
 
     theirs = (1 - zp) * 2 + c
     for part in range(4):
@@ -266,11 +278,6 @@
         here = atm.at[pl.ds(part * 192, 192), frames_of(theirs)]
         swaps.append(send(here, here, sem_a_s.at[6 + part], sem_a_r.at[6 + part], mate))
 
-    for side in range(2):
-        here = rows_of(y_far, xl, side)
-        landed(here, 4 + side)
-        push(here, 12 + side, along_x(x_step[side]))
-
     for item in u_swaps + swaps:
         item.wait_recv()
 
@@ -279,6 +286,7 @@
         value = jnp.dot(atm[rows, :], ub[:, start:start + width], preferred_element_type=F32)
         return value.reshape(4, 48, width).astype(BF16)
 
+    loads[2].wait()
     y_first = []
     for i in (1, 3, 2, 0):
         to_y = (y + i) % 4
@@ -312,20 +320,6 @@
             send(agp.at[oc, :, cols], agr.at[:, cols], sem_c_s.at[6 + k], sem_c_r.at[6 + k], mate)
         )
 
-    for item in a_swaps:
-        item.wait_recv()
-
-    def project_chunk(n, _):
-        cols = pl.ds(pl.multiple_of(n * 256, 256), 256)
-        value = jnp.dot(ab[...], wb[:, cols], preferred_element_type=F32).astype(BF16)
-        pj[0, :, cols] = value[:T]
-        pj[1, :, cols] = value[T:]
-        return 0
-
-    lax.fori_loop(0, 3, project_chunk, 0)
-    pj_swap = send(pj.at[oc], pjr, sem_c_s.at[10], sem_c_r.at[10], mate)
-    proj_ref[:, half(c)] = pj[c]
-
     for item in ag_swaps:
         item.wait_recv()
 
@@ -344,28 +338,11 @@
     ]
     inv_live = inv * live
 
-    def conv_grad_chunk(k, _):
-        at_lanes = lanes_of(k)
-        cg[PAD:PAD + T, at_lanes] = inv_live * (ds[:, at_lanes] - first - cv[:, at_lanes] * second)
-        return 0
-
-    lax.fori_loop(0, CHUNKS, conv_grad_chunk, 0)
-
-    g_before = copy(cg.at[pl.ds(PAD, PAD)], cg.at[pl.ds(PAD + T, PAD)], sem_halo_s.at[2], sem_halo_r.at[3], before)
-    g_after = copy(cg.at[pl.ds(T, PAD)], cg.at[pl.ds(0, PAD)], sem_halo_s.at[3], sem_halo_r.at[2], after)
-
-    @pl.when(t > 0)
-    def _():
-        g_before.start()
-
-    @pl.when(t < 31)
-    def _():
-        g_after.start()
-
     def taps_chunk(k, _):
         at_lanes = lanes_of(k)
         source = xf[:, at_lanes]
-        grad = cg[PAD:PAD + T, at_lanes]
+        grad = inv_live * (ds[:, at_lanes] - first - cv[:, at_lanes] * second)
+        cg[PAD:PAD + T, at_lanes] = grad
         for r in range(8):
             shifted = source[r:r + T + 24]
             for j in range(4):
@@ -377,6 +354,16 @@
     lax.fori_loop(oc * 6, oc * 6 + 6, taps_chunk, 0)
     gk_swap = send(gkb.at[:, half(oc)], gcr, sem_t_s.at[0], sem_t_r.at[0], mate)
     lax.fori_loop(c * 6, c * 6 + 6, taps_chunk, 0)
+    g_before = copy(cg.at[pl.ds(PAD, PAD)], cg.at[pl.ds(PAD + T, PAD)], sem_halo_s.at[2], sem_halo_r.at[3], before)
+    g_after = copy(cg.at[pl.ds(T, PAD)], cg.at[pl.ds(0, PAD)], sem_halo_s.at[3], sem_halo_r.at[2], after)
+
+    @pl.when(t > 0)
+    def _():
+        g_before.start()
+
+    @pl.when(t < 31)
+    def _():
+        g_after.start()
 
     def piece(z_):
         return (
@@ -415,6 +402,20 @@
         for i in (2, 1, 3)
     ]
 
+    for item in a_swaps:
+        item.wait_recv()
+
+    def project_chunk(n, _):
+        cols = pl.ds(pl.multiple_of(n * 256, 256), 256)
+        value = jnp.dot(ab[...], wb[:, cols], preferred_element_type=F32).astype(BF16)
+        pj[0, :, cols] = value[:T]
+        pj[1, :, cols] = value[T:]
+        return 0
+
+    lax.fori_loop(0, 3, project_chunk, 0)
+    pj_swap = send(pj.at[oc], pjr, sem_c_s.at[10], sem_c_r.at[10], mate)
+    proj_ref[:, half(c)] = pj[c]
+
     @pl.when(t > 0)
     def _():
         g_after.wait_recv()
@@ -444,14 +445,11 @@
     mine_t = gh[piece(z)]
     for i in range(7):
         mine_t = mine_t + zr[i]
-    xs[x] = mine_t
-    for i in (2, 1, 3):
-        send(xs.at[x], xs.at[x], sem_t_s.at[7 + i], sem_t_r.at[7 + i], along_x(i))
-
-    def wait_slots(slots, me, base):
-        for i in range(1, 4):
-            slot = slots.at[(me + 4 - i) % 4]
-            copy(slot, slot, sem_t_s.at[base + i], sem_t_r.at[base + i], mate).wait_recv()
+    xs[y * 4 + x] = mine_t
+    for i in (10, 9, 11, 6, 14, 2, 8, 5, 7, 13, 15, 1, 3, 4, 12):
+        here = xs.at[y * 4 + x]
+        to = dev((y + i // 4) % 4, (x + i % 4) % 4, z, c)
+        send(here, here, sem_t_s.at[7 + i], sem_t_r.at[7 + i], to)
 
     for item in x_second + y_second:
         item.wait_recv()
@@ -469,16 +467,17 @@
         for i in (2, 1, 3)
     ]
 
-    wait_slots(xs, x, 7)
-    ys[y] = xs[0] + xs[1] + xs[2] + xs[3]
-    for i in (2, 1, 3):
-        send(ys.at[y], ys.at[y], sem_t_s.at[10 + i], sem_t_r.at[10 + i], along_y(i))
     lax.fori_loop(6, CHUNKS, input_chunk, 0)
-    wait_slots(ys, y, 10)
-    fg[piece(z)] = ys[0] + ys[1] + ys[2] + ys[3]
+    for i in range(1, 16):
+        slot = xs.at[(y + 4 - i // 4) % 4 * 4 + (x + 4 - i % 4) % 4]
+        copy(slot, slot, sem_t_s.at[7 + i], sem_t_r.at[7 + i], mate).wait_recv()
+    total = xs[0]
+    for i in range(1, 16):
+        total = total + xs[i]
+    fg[piece(z)] = total
     for i in (4, 3, 5, 2, 6, 1, 7):
         here = fg.at[piece(z)]
-        send(here, here, sem_t_s.at[13 + i], sem_t_r.at[13 + i], along_z(i))
+        send(here, here, sem_t_s.at[22 + i], sem_t_r.at[22 + i], along_z(i))
 
     stores = [pltpu.make_async_copy(gin_ref, gin_hbm, sem_out.at[0])]
     stores[0].start()
@@ -499,8 +498,8 @@
 
     for i in range(1, 8):
         slot = fg.at[piece((z + 8 - i) % 8)]
-        copy(slot, slot, sem_t_s.at[13 + i], sem_t_r.at[13 + i], mate).wait_recv()
-    t_swap = send(fg, fgr, sem_t_s.at[21], sem_t_r.at[21], mate)
+        copy(slot, slot, sem_t_s.at[22 + i], sem_t_r.at[22 + i], mate).wait_recv()
+    t_swap = send(fg, fgr, sem_t_s.at[30], sem_t_r.at[30], mate)
 
     def put_taps(cols, value):
         gk_ref[:, cols] = value[0:TAPS]
@@ -533,14 +532,17 @@
 
 
 def deliver(*refs):
-    sources, results, kept, sems = refs[:5], refs[5:10], refs[10:15], refs[15]
+    sources, results, kept, flat, sems = refs[:5], refs[5:10], refs[10:15], refs[15], refs[16]
     loads = [pltpu.make_async_copy(a, b, sems.at[n]) for n, (a, b) in enumerate(zip(sources, kept))]
-    stores = [pltpu.make_async_copy(a, b, sems.at[5 + n]) for n, (a, b) in enumerate(zip(kept, results))]
+    stores = [pltpu.make_async_copy(a, b, sems.at[5 + n]) for n, (a, b) in enumerate(zip(kept[:4] + (flat,), results))]
     for item in loads:
         item.start()
-    for first, then in zip(loads, stores):
+    for first, then in zip(loads[:4], stores):
         first.wait()
         then.start()
+    loads[4].wait()
+    flat[...] = kept[4][0]
+    stores[4].start()
     for item in stores:
         item.wait()
 
@@ -595,8 +597,7 @@
         pltpu.VMEM((32, H), F32),
         pltpu.VMEM((32, H), F32),
         pltpu.VMEM((7, 8, 384), F32),
-        pltpu.VMEM((4, 8, 384), F32),
-        pltpu.VMEM((4, 8, 384), F32),
+        pltpu.VMEM((16, 8, 384), F32),
         pltpu.VMEM((32, H), F32),
         pltpu.VMEM((32, H), F32),
         dma((4,)), dma((4,)),
@@ -604,7 +605,7 @@
         dma((12,)), dma((12,)),
         dma((12,)), dma((12,)),
         dma((8,)), dma((8,)),
-        dma((22,)), dma((22,)),
+        dma((31,)), dma((31,)),
         dma((10,)), dma((10,)),
         dma((6,)), dma((5,)),
     ]
@@ -629,14 +630,14 @@
     )(inputs[0], lengths, kernel, norm_gain, weight, cotangent[0])
     projected, grad_input, grad_weight, grad_kernel, grad_gain = pl.pallas_call(
         deliver,
-        out_shape=shapes,
+        out_shape=shapes[:4] + (jax.ShapeDtypeStruct((D,), F32),),
         in_specs=[hbm] * 5,
         out_specs=[hbm] * 5,
-        scratch_shapes=[pltpu.VMEM(r.shape, r.dtype) for r in shapes] + [dma((10,))],
+        scratch_shapes=[pltpu.VMEM(r.shape, r.dtype) for r in shapes] + [pltpu.VMEM((D,), F32), dma((10,))],
         compiler_params=pltpu.CompilerParams(vmem_limit_bytes=60 << 20),
         name="deliver",
     )(*results)
-    return (projected[None], grad_input[None], grad_weight, grad_kernel, grad_gain[0])
+    return (projected[None], grad_input[None], grad_weight, grad_kernel, grad_gain)
 
 
 def solution(mesh):

time: 60.7 us -> 58.1 us (0.957)
  Pallas kernels: 57.9 us -> 56.7 us
  local copies, waits for them, and re-layouts: 0.69 us -> 0 us
  other arithmetic: 0.62 us -> 0 us
    pallas_call x1, Pallas kernels: 55.9 us -> 54.7 us  [on_device(): pl.pallas_call(fused, out_shape=shapes, in_specs=[hbm] * 6, out_specs=[hb...]
    unnamed x2 -> x0, local copies, waits for them, and re-layouts: 0.69 us -> none
    pallas_call x1 -> x0, other arithmetic: 0.62 us -> none  [on_device(): pl.pallas_call(deliver, out_shape=shapes, in_specs=[hbm] * 5, out_specs=[...]
where the time goes in v1:
time: 58.1 us; the launch traced here: 58 us
  Pallas kernels  56.7 us (98%)
  between operations  1.29 us (2%)
    pallas_call x1, Pallas kernels, on_device(): pl.pallas_call(fused, out_shape=shapes, in_specs=[hbm] * 6, out_specs=[hb...  54.7 us
    pallas_call x1, Pallas kernels, on_device(): pl.pallas_call(deliver, out_shape=shapes[:4] + (jax.ShapeDtypeStruct((D,)...  2.04 us

profile of v1, /device:TPU:1, one launch (start us, length us, event | category | flops | bytes accessed | tf_op | source)
XLA Modules:
  0.0 58.0 jit_solution(17649068829314252671)
XLA Ops:
  1.3 54.7 %conv_module.1 = (bf16[128,1536]{1,0:T(8,128)(2,1)}, bf16[128,1536]{1,0:T(8,128)(2,1)}, f32[6,1536]{1,0:T(8,128)}, f32[31,1536]{1,0:T(8,128)}, f32[1,1536]{1,0:T(1,128)}) custom-call(bf16[128,1536]{1,0:T(8,128)(2,1)} %bitcast.4, s32[1]{0:T(128)S(6)} %copy.11.len_hbm, f32[31,1536]{1,0:T(8,128)} %kern_hbm.1, f32[1536]{0:T(1024)} %gain_hbm.1, ...), custom_call_target="tpu_custom_call" | custom-call | tf_op jit(solution)/shard_map/conv_module/pallas_call | solution.py:620
  56.0 2.0 %deliver.1 = (bf16[128,1536]{1,0:T(8,128)(2,1)}, bf16[128,1536]{1,0:T(8,128)(2,1)}, f32[6,1536]{1,0:T(8,128)}, f32[31,1536]{1,0:T(8,128)}, f32[1536]{0:T(1024)}) custom-call(bf16[128,1536]{1,0:T(8,128)(2,1)} %get-tuple-element.15.refs_0_, bf16[128,1536]{1,0:T(8,128)(2,1)} %get-tuple-element.16.refs_1_, f32[6,1536]{1,0:T(8,128)} %get-tuple-element.17.refs_2_, ...), custom_call_target="tpu_custom_call" | custom-call | tf_op jit(solution)/shard_map/deliver/pallas_call | solution.py:631

commit v2 on v1

--- a/solution.py
+++ b/solution.py
@@ -9,7 +9,7 @@
 MESH = pl.DeviceIdType.MESH
 D, T, H, TAPS = 1536, 128, 768, 31
 PAD = 16
-CX, CY = 384, 384
+CX, CY = 256, 512
 LANES = 128
 CHUNKS = D // LANES
 
@@ -21,41 +21,46 @@
 def fused(
     x_hbm, len_hbm, kern_hbm, gain_hbm, w_hbm, cot_hbm,
     proj_hbm, gin_hbm, gw_hbm, gk_hbm, gg_hbm,
-    len_ref, x_ref, kern_ref, gain_ref, cot_ref, proj_ref, gin_ref, gw_ref, gk_ref, gg_ref,
-    xm, hx, xf, cv, ds, rs_sum, ab, tf, tp, at2, atm, us, ub, wb, px, py, rx, ry, s2x, s2y, r2x, r2y,
-    facc, zs, rz, fin, cr, agp, agr, pj, pjr, cg, gkb, gcr, gh, zr, xs, fg, fgr,
+    len_ref, x_ref, kern_ref, gain_ref, proj_ref, gin_ref, gw_ref, gk_ref, gg_ref,
+    hx, xf, cv, ds, rs_sum, ab, tf, tp, at2, atm, ub, wb, px, py, rx, ry, s2x, s2y, r2x, r2y,
+    facc, zs, rz, fin, cr, agp, agr, pj, pjr, cg, gkb, gcr, gh, gp, zr, xs, fg, fgr,
     sem_halo_s, sem_halo_r, sem_w_s, sem_w_r, sem_c_s, sem_c_r, sem_p_s, sem_p_r,
     sem_z_s, sem_z_r, sem_t_s, sem_t_r, sem_a_s, sem_a_r, sem_in, sem_out,
 ):
     b = lax.axis_index("batch")
     t = lax.axis_index("tm")
-    y, xl = b // 2, b % 2
-    xh, z, c = t // 16, (t // 2) % 8, t % 2
+    y, xl = lax.div(b, 2), lax.rem(b, 2)
+    xh, z, c = lax.div(t, 16), lax.rem(lax.div(t, 2), 8), lax.rem(t, 2)
     x = xh * 2 + xl
     oc = 1 - c
 
-    def dev(y_, x_, z_, c_):
-        return (y_ * 2 + x_ % 2, (x_ // 2) * 16 + z_ * 2 + c_)
+    ys = [y] + [lax.rem(y + i, 4) for i in range(1, 4)]
+    xr = [x] + [lax.rem(x + i, 4) for i in range(1, 4)]
+    zr_ = [z] + [lax.rem(z + i, 8) for i in range(1, 8)]
+    low, high = [lax.rem(v, 2) for v in xr], [lax.div(v, 2) for v in xr]
+    blocks = [l * 2 + h for l, h in zip(low, high)]
+
+    def dev(dy, dx, z_, c_):
+        return (ys[dy] * 2 + low[dx], high[dx] * 16 + z_ * 2 + c_)
 
     def along_y(i):
-        return dev((y + i) % 4, x, z, c)
+        return dev(i, 0, z, c)
 
     def along_x(i):
-        return dev(y, (x + i) % 4, z, c)
+        return dev(0, i, z, c)
 
     def along_z(i):
-        return dev(y, x, (z + i) % 8, c)
-
-    mate = dev(y, x, z, oc)
-    zp = z % 2
+        return dev(0, 0, zr_[i], c)
+
+    mate = dev(0, 0, z, oc)
+    zp = lax.rem(z, 2)
+    zh = lax.div(z, 2)
+    zhs = [zh] + [lax.rem(zh + i, 4) for i in range(1, 4)]
     z_mate = z + 1 - 2 * zp
-    across, diagonal = dev(y, x, z_mate, c), dev(y, x, z_mate, oc)
+    across, diagonal = dev(0, 0, z_mate, c), dev(0, 0, z_mate, oc)
     before, after = (b, t - 1), (b, t + 1)
 
-    def block_of(x_):
-        return (x_ % 2) * 2 + x_ // 2
-
-    q = block_of(x)
+    q = blocks[0]
 
     def half(c_):
         return pl.ds(pl.multiple_of(c_ * H, H), H)
@@ -84,7 +89,7 @@
     greet(mate)
     greet(diagonal)
     for i in range(1, 16):
-        greet(dev((y + i // 4) % 4, (x + i % 4) % 4, z, c))
+        greet(dev(i // 4, i % 4, z, c))
     for i in range(1, 8):
         greet(along_z(i))
 
@@ -96,11 +101,12 @@
     def _():
         greet(after)
 
+    mine = zp * 2 + c
     w_own = pl.ds(pl.multiple_of((y * 2 + xl) * 192, 192), 192)
     loads = [
         pltpu.make_async_copy(src, dst, sem_in.at[n])
         for n, (src, dst) in enumerate((
-            (x_hbm, x_ref), (cot_hbm, cot_ref), (w_hbm.at[:, half(c)], wb.at[w_own]),
+            (x_hbm, x_ref), (cot_hbm.at[:, half(c)], ub.at[frames_of(mine)]), (w_hbm.at[:, half(c)], wb.at[w_own]),
             (kern_hbm, kern_ref), (gain_hbm, gain_ref), (len_hbm, len_ref),
         ))
     ]
@@ -109,10 +115,30 @@
     others = 24 + jnp.where(t > 0, 1, 0) + jnp.where(t < 31, 1, 0)
     pl.semaphore_wait(barrier, others)
 
+    to_before = copy(x_hbm.at[pl.ds(0, PAD)], hx.at[1], sem_halo_s.at[0], sem_halo_r.at[1], before)
+    to_after = copy(x_hbm.at[pl.ds(T - PAD, PAD)], hx.at[0], sem_halo_s.at[1], sem_halo_r.at[0], after)
+
+    @pl.when(t > 0)
+    def _():
+        to_before.start()
+
+    @pl.when(t < 31)
+    def _():
+        to_after.start()
+
+    u_swaps = [
+        send(cot_hbm.at[:, half(c_)], ub.at[frames_of(mine)], ss, rs, to)
+        for c_, ss, rs, to in (
+            (oc, sem_c_s.at[0], sem_c_r.at[0], mate),
+            (c, sem_a_s.at[0], sem_a_r.at[0], across),
+            (oc, sem_a_s.at[1], sem_a_r.at[1], diagonal),
+        )
+    ]
+
     def rows_of(y_, xl_, side):
         return wb.at[pl.ds(pl.multiple_of((y_ * 2 + xl_) * 192 + side * 96, 96), 96)]
 
-    y_up, y_down, y_far = (y + 1) % 4, (y + 3) % 4, (y + 2) % 4
+    y_up, y_down, y_far = ys[1], ys[3], ys[2]
     x_step = (1, 3)
 
     def push(here, n, to):
@@ -134,38 +160,15 @@
     loads[5].wait()
     position = t * T + lax.broadcasted_iota(jnp.int32, (T, LANES), 0)
     live = jnp.where(position < len_ref[0], 1.0, 0.0).astype(F32)
-    for item in loads[:2]:
-        item.wait()
+    loads[0].wait()
 
     def mask_chunk(k, _):
         at_lanes = lanes_of(k)
         masked = x_ref[:, at_lanes].astype(F32) * live
-        xm[:, at_lanes] = masked.astype(BF16)
         xf[PAD:PAD + T, at_lanes] = masked
-        us[:, at_lanes] = (cot_ref[:, at_lanes].astype(F32) * live).astype(BF16)
         return 0
 
     lax.fori_loop(0, CHUNKS, mask_chunk, 0)
-
-    to_before = copy(xm.at[pl.ds(0, PAD)], hx.at[1], sem_halo_s.at[0], sem_halo_r.at[1], before)
-    to_after = copy(xm.at[pl.ds(T - PAD, PAD)], hx.at[0], sem_halo_s.at[1], sem_halo_r.at[0], after)
-
-    @pl.when(t > 0)
-    def _():
-        to_before.start()
-
-    @pl.when(t < 31)
-    def _():
-        to_after.start()
-
-    mine = zp * 2 + c
-    u_swaps = [send(us.at[:, half(oc)], ub.at[frames_of(mine)], sem_c_s.at[0], sem_c_r.at[0], mate)]
-
-    u_swaps += [
-        send(us.at[:, half(c_)], ub.at[frames_of(mine)], sem_a_s.at[n], sem_a_r.at[n], to)
-        for n, c_, to in ((0, c, across), (1, oc, diagonal))
-    ]
-    ub[frames_of(mine), :] = us[:, half(c)]
 
     for item in loads[3:5]:
         item.wait()
@@ -196,10 +199,15 @@
 
     conv_chunk(PAD, T - 2 * PAD)
 
+    def alive_halo(side, row, frame):
+        frames = frame + lax.broadcasted_iota(jnp.int32, (PAD, D), 0)
+        alive = jnp.where(frames < len_ref[0], 1.0, 0.0).astype(F32)
+        xf[row:row + PAD, :] = hx[side].astype(F32) * alive
+
     @pl.when(t > 0)
     def _():
         to_after.wait_recv()
-        xf[0:PAD, :] = hx[0].astype(F32)
+        alive_halo(0, 0, t * T - PAD)
 
     @pl.when(t == 0)
     def _():
@@ -208,7 +216,7 @@
     @pl.when(t < 31)
     def _():
         to_before.wait_recv()
-        xf[PAD + T:, :] = hx[1].astype(F32)
+        alive_halo(1, PAD + T, t * T + T)
 
     @pl.when(t == 31)
     def _():
@@ -238,7 +246,7 @@
         cv[:, at_lanes] = normed
         ds[:, at_lanes] = gate * (1.0 + scaled * (1.0 - gate))
         ab[frames_of(c), at_lanes] = act.astype(BF16)
-        tf[pl.ds(pl.multiple_of((k % 3) * LANES, LANES), LANES), :] = act.T
+        tf[pl.ds(pl.multiple_of(lax.rem(k, 3) * LANES, LANES), LANES), :] = act.T
         return 0
 
     def pass_on(*pieces):
@@ -272,13 +280,28 @@
         landed(here, 4 + side)
         push(here, 12 + side, along_x(x_step[side]))
 
+    loads[1].wait()
+    loads[2].wait()
+    for item in u_swaps:
+        item.wait_recv()
+    for slot in range(4):
+        first_frame = (xh * 16 + (z - zp) * 2 + slot) * T
+        alive = jnp.where(position - t * T + first_frame < len_ref[0], 1.0, 0.0).astype(F32)
+
+        def mask_upstream(k, _):
+            rows, at_lanes = slice(slot * T, slot * T + T), lanes_of(k)
+            ub[rows, at_lanes] = (ub[rows, at_lanes].astype(F32) * alive).astype(BF16)
+            return 0
+
+        lax.fori_loop(0, H // LANES, mask_upstream, 0)
+
     theirs = (1 - zp) * 2 + c
     for part in range(4):
         z_swaps[part].wait_recv()
         here = atm.at[pl.ds(part * 192, 192), frames_of(theirs)]
         swaps.append(send(here, here, sem_a_s.at[6 + part], sem_a_r.at[6 + part], mate))
 
-    for item in u_swaps + swaps:
+    for item in swaps:
         item.wait_recv()
 
     def partial(n, start, width):
@@ -286,10 +309,9 @@
         value = jnp.dot(atm[rows, :], ub[:, start:start + width], preferred_element_type=F32)
         return value.reshape(4, 48, width).astype(BF16)
 
-    loads[2].wait()
     y_first = []
     for i in (1, 3, 2, 0):
-        to_y = (y + i) % 4
+        to_y = ys[i]
         py[to_y] = partial(to_y, CX, CY)
         if i:
             y_first.append(send(py.at[to_y], ry.at[i - 1], sem_p_s.at[2 + i], sem_p_r.at[2 + i], along_y(i)))
@@ -300,7 +322,7 @@
 
     lax.fori_loop(0, 4, partial_x, 0)
     x_first = [
-        send(px.at[:, block_of((x + i) % 4)], rx.at[i - 1], sem_p_s.at[i - 1], sem_p_r.at[i - 1], along_x(i))
+        send(px.at[:, blocks[i]], rx.at[i - 1], sem_p_s.at[i - 1], sem_p_r.at[i - 1], along_x(i))
         for i in (1, 3, 2)
     ]
 
@@ -365,18 +387,26 @@
     def _():
         g_after.start()
 
-    def piece(z_):
-        return (
-            pl.ds(pl.multiple_of((z_ // 2) * 8, 8), 8),
-            pl.ds(pl.multiple_of((z_ % 2) * 384, 384), 384),
-        )
+    def pieces():
+        for n in range(16):
+            yield n, slice(n // 4 * 8, n // 4 * 8 + 8), slice(n % 4 * 192, n % 4 * 192 + 192)
+
+    plane = (10, 9, 11, 6, 14, 2, 8, 5, 7, 13, 15, 1, 3, 4, 12)
+    line = (4, 3, 5, 2, 6, 1, 7)
+    here = y * 4 + x
+
+    def in_plane(i):
+        return ys[i // 4] * 4 + xr[i % 4], dev(i // 4, i % 4, z, c)
 
     gk_swap.wait_recv()
     gh[...] = gkb[:, half(c)] + gcr[...]
-    t_z = [
-        send(gh.at[piece((z + i) % 8)], zr.at[i - 1], sem_t_s.at[i], sem_t_r.at[i], along_z(i))
-        for i in (4, 3, 5, 2, 6, 1, 7)
-    ]
+    gp[...] = jnp.zeros((16, 8, 256), F32)
+    for n, rows, cols in pieces():
+        gp[n, :, 0:192] = gh[rows, cols]
+    t_plane = []
+    for i in plane:
+        n, to = in_plane(i)
+        t_plane.append(send(gp.at[n], zr.at[i - 1], sem_t_s.at[i], sem_t_r.at[i], to))
 
     def add(first, own, came, out):
         for item in first:
@@ -393,12 +423,12 @@
 
     add(x_first, lambda n: px[n, q], rx, s2x)
     x_second = [
-        send(s2x.at[(y + i) % 4], r2x.at[i - 1], sem_p_s.at[5 + i], sem_p_r.at[5 + i], along_y(i))
+        send(s2x.at[ys[i]], r2x.at[i - 1], sem_p_s.at[5 + i], sem_p_r.at[5 + i], along_y(i))
         for i in (2, 1, 3)
     ]
     add(y_first, lambda n: py[y, n], ry, s2y)
     y_second = [
-        send(s2y.at[block_of((x + i) % 4)], r2y.at[i - 1], sem_p_s.at[8 + i], sem_p_r.at[8 + i], along_x(i))
+        send(s2y.at[blocks[i]], r2y.at[i - 1], sem_p_s.at[8 + i], sem_p_r.at[8 + i], along_x(i))
         for i in (2, 1, 3)
     ]
 
@@ -440,16 +470,15 @@
 
     lax.fori_loop(0, 6, input_chunk, 0)
 
-    for item in t_z:
+    for item in t_plane:
         item.wait_recv()
-    mine_t = gh[piece(z)]
-    for i in range(7):
-        mine_t = mine_t + zr[i]
-    xs[y * 4 + x] = mine_t
-    for i in (10, 9, 11, 6, 14, 2, 8, 5, 7, 13, 15, 1, 3, 4, 12):
-        here = xs.at[y * 4 + x]
-        to = dev((y + i // 4) % 4, (x + i % 4) % 4, z, c)
-        send(here, here, sem_t_s.at[7 + i], sem_t_r.at[7 + i], to)
+    total = gp[here]
+    for i in range(15):
+        total = total + zr[i]
+    xs[z] = total
+    for i in line:
+        slot = xs.at[z]
+        send(slot, slot, sem_t_s.at[15 + i], sem_t_r.at[15 + i], along_z(i))
 
     for item in x_second + y_second:
         item.wait_recv()
@@ -463,21 +492,20 @@
     for n in range(4):
         zs[n] = facc[12 * n:12 * n + 16, :].astype(BF16)
     w_z = [
-        send(zs.at[(z // 2 + i) % 4], rz.at[i - 1], sem_z_s.at[i - 1], sem_z_r.at[i - 1], along_z(2 * i))
+        send(zs.at[zhs[i]], rz.at[i - 1], sem_z_s.at[i - 1], sem_z_r.at[i - 1], along_z(2 * i))
         for i in (2, 1, 3)
     ]
 
     lax.fori_loop(6, CHUNKS, input_chunk, 0)
-    for i in range(1, 16):
-        slot = xs.at[(y + 4 - i // 4) % 4 * 4 + (x + 4 - i % 4) % 4]
-        copy(slot, slot, sem_t_s.at[7 + i], sem_t_r.at[7 + i], mate).wait_recv()
+    for i in range(1, 8):
+        slot = xs.at[zr_[8 - i]]
+        copy(slot, slot, sem_t_s.at[15 + i], sem_t_r.at[15 + i], mate).wait_recv()
     total = xs[0]
-    for i in range(1, 16):
+    for i in range(1, 8):
         total = total + xs[i]
-    fg[piece(z)] = total
-    for i in (4, 3, 5, 2, 6, 1, 7):
-        here = fg.at[piece(z)]
-        send(here, here, sem_t_s.at[22 + i], sem_t_r.at[22 + i], along_z(i))
+    fg[here] = total
+    for i in plane:
+        send(fg.at[here], fg.at[here], sem_t_s.at[22 + i], sem_t_r.at[22 + i], in_plane(i)[1])
 
     stores = [pltpu.make_async_copy(gin_ref, gin_hbm, sem_out.at[0])]
     stores[0].start()
@@ -488,7 +516,7 @@
 
     for item in w_z:
         item.wait_recv()
-    rows = zs[z // 2].astype(F32)
+    rows = zs[zh].astype(F32)
     for i in range(3):
         rows = rows + rz[i].astype(F32)
     fin[...] = jnp.zeros((2, 8, H), F32)
@@ -496,19 +524,21 @@
     fin[1, 0:6, :] = rows[6:12]
     w_swap = send(fin.at[oc], cr, sem_z_s.at[3], sem_z_r.at[3], mate)
 
-    for i in range(1, 8):
-        slot = fg.at[piece((z + 8 - i) % 8)]
+    for i in range(1, 16):
+        slot = fg.at[ys[-(i // 4) % 4] * 4 + xr[-(i % 4) % 4]]
         copy(slot, slot, sem_t_s.at[22 + i], sem_t_r.at[22 + i], mate).wait_recv()
-    t_swap = send(fg, fgr, sem_t_s.at[30], sem_t_r.at[30], mate)
-
-    def put_taps(cols, value):
-        gk_ref[:, cols] = value[0:TAPS]
-        gg_ref[:, cols] = value[TAPS:TAPS + 1]
-
-    put_taps(half(c), fg[...])
+    t_swap = send(fg, fgr, sem_t_s.at[38], sem_t_r.at[38], mate)
+
+    def put_taps(cols, source):
+        for n, rows, part in pieces():
+            gh[rows, part] = source[n, :, 0:192]
+        gk_ref[:, cols] = gh[0:TAPS, :]
+        gg_ref[:, cols] = gh[TAPS:TAPS + 1, :]
+
+    put_taps(half(c), fg)
     gw_ref[:, half(c)] = fin[c][0:6]
     t_swap.wait_recv()
-    put_taps(half(oc), fgr[...])
+    put_taps(half(oc), fgr)
     w_swap.wait_recv()
     gw_ref[:, half(oc)] = cr[0:6, :]
     for n, (src, dst) in enumerate(((gw_ref, gw_hbm), (gk_ref, gk_hbm), (gg_ref, gg_hbm))):
@@ -557,11 +587,9 @@
         pltpu.VMEM((D,), F32),
         pltpu.VMEM((T, D), BF16),
         pltpu.VMEM((T, D), BF16),
-        pltpu.VMEM((T, D), BF16),
         pltpu.VMEM((6, D), F32),
         pltpu.VMEM((TAPS, D), F32),
         pltpu.VMEM((1, D), F32),
-        pltpu.VMEM((T, D), BF16),
         pltpu.VMEM((2, PAD, D), BF16),
         pltpu.VMEM((T + 2 * PAD, D), F32),
         pltpu.VMEM((T, D), F32),
@@ -572,7 +600,6 @@
         pltpu.VMEM((192, T), F32),
         pltpu.VMEM((2, H, T), BF16),
         pltpu.VMEM((H, 4 * T), BF16),
-        pltpu.VMEM((T, D), BF16),
         pltpu.VMEM((4 * T, H), BF16),
         pltpu.VMEM((D, H), BF16),
         pltpu.VMEM((4, 4, 48, CX), BF16),
@@ -596,16 +623,17 @@
         pltpu.VMEM((32, D), F32),
         pltpu.VMEM((32, H), F32),
         pltpu.VMEM((32, H), F32),
-        pltpu.VMEM((7, 8, 384), F32),
-        pltpu.VMEM((16, 8, 384), F32),
-        pltpu.VMEM((32, H), F32),
-        pltpu.VMEM((32, H), F32),
+        pltpu.VMEM((16, 8, 256), F32),
+        pltpu.VMEM((15, 8, 256), F32),
+        pltpu.VMEM((8, 8, 256), F32),
+        pltpu.VMEM((16, 8, 256), F32),
+        pltpu.VMEM((16, 8, 256), F32),
         dma((4,)), dma((4,)),
         dma((14,)), dma((14,)),
         dma((12,)), dma((12,)),
         dma((12,)), dma((12,)),
         dma((8,)), dma((8,)),
-        dma((31,)), dma((31,)),
+        dma((39,)), dma((39,)),
         dma((10,)), dma((10,)),
         dma((6,)), dma((5,)),
     ]

time: 58.1 us -> 57 us (0.981)
  Pallas kernels: 56.7 us -> 55.6 us
    pallas_call x1, Pallas kernels: 54.7 us -> 53.6 us  [on_device(): pl.pallas_call(fused, out_shape=shapes, in_specs=[hbm] * 6, out_specs=[hb...]
where the time goes in v2:
time: 57 us; the launch traced here: 56.9 us
  Pallas kernels  55.6 us (98%)
  between operations  1.29 us (2%)
    pallas_call x1, Pallas kernels, on_device(): pl.pallas_call(fused, out_shape=shapes, in_specs=[hbm] * 6, out_specs=[hb...  53.6 us
    pallas_call x1, Pallas kernels, on_device(): pl.pallas_call(deliver, out_shape=shapes[:4] + (jax.ShapeDtypeStruct((D,)...  2.04 us

profile of v2, /device:TPU:1, one launch (start us, length us, event | category | flops | bytes accessed | tf_op | source)
XLA Modules:
  0.0 56.9 jit_solution(12462023793435331622)
XLA Ops:
  1.3 53.6 %conv_module.1 = (bf16[128,1536]{1,0:T(8,128)(2,1)}, bf16[128,1536]{1,0:T(8,128)(2,1)}, f32[6,1536]{1,0:T(8,128)}, f32[31,1536]{1,0:T(8,128)}, f32[1,1536]{1,0:T(1,128)}) custom-call(bf16[128,1536]{1,0:T(8,128)(2,1)} %bitcast.4, s32[1]{0:T(128)S(6)} %copy.11.len_hbm, f32[31,1536]{1,0:T(8,128)} %kern_hbm.1, f32[1536]{0:T(1024)} %gain_hbm.1, ...), custom_call_target="tpu_custom_call" | custom-call | tf_op jit(solution)/shard_map/conv_module/pallas_call | solution.py:648
  54.8 2.0 %deliver.1 = (bf16[128,1536]{1,0:T(8,128)(2,1)}, bf16[128,1536]{1,0:T(8,128)(2,1)}, f32[6,1536]{1,0:T(8,128)}, f32[31,1536]{1,0:T(8,128)}, f32[1536]{0:T(1024)}) custom-call(bf16[128,1536]{1,0:T(8,128)(2,1)} %get-tuple-element.15.refs_0_, bf16[128,1536]{1,0:T(8,128)(2,1)} %get-tuple-element.16.refs_1_, f32[6,1536]{1,0:T(8,128)} %get-tuple-element.17.refs_2_, ...), custom_call_target="tpu_custom_call" | custom-call | tf_op jit(solution)/shard_map/deliver/pallas_call | solution.py:659

commit v3 on v2

--- a/solution.py
+++ b/solution.py
@@ -25,7 +25,7 @@
     hx, xf, cv, ds, rs_sum, ab, tf, tp, at2, atm, ub, wb, px, py, rx, ry, s2x, s2y, r2x, r2y,
     facc, zs, rz, fin, cr, agp, agr, pj, pjr, cg, gkb, gcr, gh, gp, zr, xs, fg, fgr,
     sem_halo_s, sem_halo_r, sem_w_s, sem_w_r, sem_c_s, sem_c_r, sem_p_s, sem_p_r,
-    sem_z_s, sem_z_r, sem_t_s, sem_t_r, sem_a_s, sem_a_r, sem_in, sem_out,
+    sem_z_s, sem_z_r, sem_t_s, sem_t_r, sem_a_s, sem_a_r, sem_in, sem_out, sem_far,
 ):
     b = lax.axis_index("batch")
     t = lax.axis_index("tm")
@@ -81,6 +81,15 @@
         started.append(item)
         return item
 
+    def sent_so_far():
+        items = list(started)
+        started.clear()
+        return items
+
+    def all_sent(items):
+        for item in items:
+            item.wait_send()
+
     barrier = pltpu.get_barrier_semaphore()
 
     def greet(to):
@@ -88,10 +97,9 @@
 
     greet(mate)
     greet(diagonal)
-    for i in range(1, 16):
-        greet(dev(i // 4, i % 4, z, c))
-    for i in range(1, 8):
-        greet(along_z(i))
+    beside = [along_x(1), along_x(3), along_y(1), along_y(3), along_z(1), along_z(7)]
+    for to in beside:
+        greet(to)
 
     @pl.when(t > 0)
     def _():
@@ -112,7 +120,7 @@
     ]
     for item in loads:
         item.start()
-    others = 24 + jnp.where(t > 0, 1, 0) + jnp.where(t < 31, 1, 0)
+    others = 8 + jnp.where(t > 0, 1, 0) + jnp.where(t < 31, 1, 0)
     pl.semaphore_wait(barrier, others)
 
     to_before = copy(x_hbm.at[pl.ds(0, PAD)], hx.at[1], sem_halo_s.at[0], sem_halo_r.at[1], before)
@@ -135,6 +143,13 @@
         )
     ]
 
+    def tell(n):
+        for to in beside:
+            pl.semaphore_signal(sem_far.at[n], inc=1, device_id=to, device_id_type=MESH)
+
+    def told(n):
+        pl.semaphore_wait(sem_far.at[n], len(beside))
+
     def rows_of(y_, xl_, side):
         return wb.at[pl.ds(pl.multiple_of((y_ * 2 + xl_) * 192 + side * 96, 96), 96)]
 
@@ -156,6 +171,8 @@
         push_own(side, 6 + side, along_x(x_step[side]))
     push_own(1, 1, along_y(1))
     push_own(0, 2, along_y(3))
+
+    tell(0)
 
     loads[5].wait()
     position = t * T + lax.broadcasted_iota(jnp.int32, (T, LANES), 0)
@@ -225,6 +242,9 @@
     conv_chunk(0, PAD)
     conv_chunk(T - PAD, PAD)
 
+    told(0)
+    tell(1)
+
     zero = jnp.zeros((T, LANES), F32)
     total = rs_sum[...]
     average = jnp.broadcast_to(jnp.sum(total, axis=1, keepdims=True) * (1.0 / D), (T, LANES))
@@ -274,6 +294,9 @@
     here = ab.at[frames_of(c)]
     a_swaps.append(send(here, here, sem_c_s.at[5], sem_c_r.at[5], mate))
 
+    told(1)
+    tell(2)
+
     pass_on((2, y_up, 0), (0, y_down, 1))
     for side in range(2):
         here = rows_of(y_far, xl, side)
@@ -301,6 +324,8 @@
         here = atm.at[pl.ds(part * 192, 192), frames_of(theirs)]
         swaps.append(send(here, here, sem_a_s.at[6 + part], sem_a_r.at[6 + part], mate))
 
+    told(2)
+
     for item in swaps:
         item.wait_recv()
 
@@ -310,7 +335,7 @@
         return value.reshape(4, 48, width).astype(BF16)
 
     y_first = []
-    for i in (1, 3, 2, 0):
+    for i in (2, 1, 3, 0):
         to_y = ys[i]
         py[to_y] = partial(to_y, CX, CY)
         if i:
@@ -323,7 +348,7 @@
     lax.fori_loop(0, 4, partial_x, 0)
     x_first = [
         send(px.at[:, blocks[i]], rx.at[i - 1], sem_p_s.at[i - 1], sem_p_r.at[i - 1], along_x(i))
-        for i in (1, 3, 2)
+        for i in (2, 1, 3)
     ]
 
     ag_swaps = []
@@ -398,6 +423,7 @@
     def in_plane(i):
         return ys[i // 4] * 4 + xr[i % 4], dev(i // 4, i % 4, z, c)
 
+    early = sent_so_far()
     gk_swap.wait_recv()
     gh[...] = gkb[:, half(c)] + gcr[...]
     gp[...] = jnp.zeros((16, 8, 256), F32)
@@ -469,6 +495,7 @@
         return 0
 
     lax.fori_loop(0, 6, input_chunk, 0)
+    all_sent(early)
 
     for item in t_plane:
         item.wait_recv()
@@ -504,11 +531,24 @@
     for i in range(1, 8):
         total = total + xs[i]
     fg[here] = total
+    middle = sent_so_far()
     for i in plane:
         send(fg.at[here], fg.at[here], sem_t_s.at[22 + i], sem_t_r.at[22 + i], in_plane(i)[1])
 
     stores = [pltpu.make_async_copy(gin_ref, gin_hbm, sem_out.at[0])]
     stores[0].start()
+    all_sent(middle)
+
+    @pl.when(t > 0)
+    def _():
+        to_before.wait_send()
+        g_before.wait_send()
+
+    @pl.when(t < 31)
+    def _():
+        to_after.wait_send()
+        g_after.wait_send()
+
     pj_swap.wait_recv()
     proj_ref[:, half(oc)] = pjr[...]
     stores.append(pltpu.make_async_copy(proj_ref, proj_hbm, sem_out.at[1]))
@@ -527,6 +567,7 @@
     for i in range(1, 16):
         slot = fg.at[ys[-(i // 4) % 4] * 4 + xr[-(i % 4) % 4]]
         copy(slot, slot, sem_t_s.at[22 + i], sem_t_r.at[22 + i], mate).wait_recv()
+    late = sent_so_far()
     t_swap = send(fg, fgr, sem_t_s.at[38], sem_t_r.at[38], mate)
 
     def put_taps(cols, source):
@@ -536,6 +577,7 @@
         gg_ref[:, cols] = gh[TAPS:TAPS + 1, :]
 
     put_taps(half(c), fg)
+    all_sent(late)
     gw_ref[:, half(c)] = fin[c][0:6]
     t_swap.wait_recv()
     put_taps(half(oc), fgr)
@@ -545,18 +587,7 @@
         stores.append(pltpu.make_async_copy(src, dst, sem_out.at[2 + n]))
         stores[-1].start()
 
-    @pl.when(t > 0)
-    def _():
-        to_before.wait_send()
-        g_before.wait_send()
-
-    @pl.when(t < 31)
-    def _():
-        to_after.wait_send()
-        g_after.wait_send()
-
-    for item in started:
-        item.wait_send()
+    all_sent(started)
     for item in stores:
         item.wait()
 
@@ -636,6 +667,7 @@
         dma((39,)), dma((39,)),
         dma((10,)), dma((10,)),
         dma((6,)), dma((5,)),
+        pltpu.SemaphoreType.REGULAR((3,)),
     ]
     hbm = pl.BlockSpec(memory_space=pl.ANY)
     shapes = (

time: 57 us -> 56.4 us (0.989)
  Pallas kernels: 55.6 us -> 55 us
    pallas_call x1, Pallas kernels: 53.6 us -> 52.9 us  [on_device(): pl.pallas_call(fused, out_shape=shapes, in_specs=[hbm] * 6, out_specs=[hb...]
where the time goes in v3:
time: 56.4 us; the launch traced here: 56.2 us
  Pallas kernels  55 us (98%)
  between operations  1.29 us (2%)
    pallas_call x1, Pallas kernels, on_device(): pl.pallas_call(fused, out_shape=shapes, in_specs=[hbm] * 6, out_specs=[hb...  52.9 us
    pallas_call x1, Pallas kernels, on_device(): pl.pallas_call(deliver, out_shape=shapes[:4] + (jax.ShapeDtypeStruct((D,)...  2.04 us

profile of v3, /device:TPU:1, one launch (start us, length us, event | category | flops | bytes accessed | tf_op | source)
XLA Modules:
  0.0 56.2 jit_solution(16132583169823018232)
XLA Ops:
  1.3 52.9 %conv_module.1 = (bf16[128,1536]{1,0:T(8,128)(2,1)}, bf16[128,1536]{1,0:T(8,128)(2,1)}, f32[6,1536]{1,0:T(8,128)}, f32[31,1536]{1,0:T(8,128)}, f32[1,1536]{1,0:T(1,128)}) custom-call(bf16[128,1536]{1,0:T(8,128)(2,1)} %bitcast.4, s32[1]{0:T(128)S(6)} %copy.11.len_hbm, f32[31,1536]{1,0:T(8,128)} %kern_hbm.1, f32[1536]{0:T(1024)} %gain_hbm.1, ...), custom_call_target="tpu_custom_call" | custom-call | tf_op jit(solution)/shard_map/conv_module/pallas_call | solution.py:680
  54.2 2.0 %deliver.1 = (bf16[128,1536]{1,0:T(8,128)(2,1)}, bf16[128,1536]{1,0:T(8,128)(2,1)}, f32[6,1536]{1,0:T(8,128)}, f32[31,1536]{1,0:T(8,128)}, f32[1536]{0:T(1024)}) custom-call(bf16[128,1536]{1,0:T(8,128)(2,1)} %get-tuple-element.15.refs_0_, bf16[128,1536]{1,0:T(8,128)(2,1)} %get-tuple-element.16.refs_1_, f32[6,1536]{1,0:T(8,128)} %get-tuple-element.17.refs_2_, ...), custom_call_target="tpu_custom_call" | custom-call | tf_op jit(solution)/shard_map/deliver/pallas_call | solution.py:691

commit v4 on v3

--- a/solution.py
+++ b/solution.py
@@ -367,6 +367,20 @@
             send(agp.at[oc, :, cols], agr.at[:, cols], sem_c_s.at[6 + k], sem_c_r.at[6 + k], mate)
         )
 
+    for item in a_swaps:
+        item.wait_recv()
+
+    def project_chunk(n, _):
+        cols = pl.ds(pl.multiple_of(n * 256, 256), 256)
+        value = jnp.dot(ab[...], wb[:, cols], preferred_element_type=F32).astype(BF16)
+        pj[0, :, cols] = value[:T]
+        pj[1, :, cols] = value[T:]
+        return 0
+
+    lax.fori_loop(0, 3, project_chunk, 0)
+    pj_swap = send(pj.at[oc], pjr, sem_c_s.at[10], sem_c_r.at[10], mate)
+    proj_ref[:, half(c)] = pj[c]
+
     for item in ag_swaps:
         item.wait_recv()
 
@@ -458,20 +472,6 @@
         for i in (2, 1, 3)
     ]
 
-    for item in a_swaps:
-        item.wait_recv()
-
-    def project_chunk(n, _):
-        cols = pl.ds(pl.multiple_of(n * 256, 256), 256)
-        value = jnp.dot(ab[...], wb[:, cols], preferred_element_type=F32).astype(BF16)
-        pj[0, :, cols] = value[:T]
-        pj[1, :, cols] = value[T:]
-        return 0
-
-    lax.fori_loop(0, 3, project_chunk, 0)
-    pj_swap = send(pj.at[oc], pjr, sem_c_s.at[10], sem_c_r.at[10], mate)
-    proj_ref[:, half(c)] = pj[c]
-
     @pl.when(t > 0)
     def _():
         g_after.wait_recv()
@@ -494,7 +494,6 @@
         gin_ref[:, at_lanes] = value.astype(BF16)
         return 0
 
-    lax.fori_loop(0, 6, input_chunk, 0)
     all_sent(early)
 
     for item in t_plane:
@@ -523,7 +522,7 @@
         for i in (2, 1, 3)
     ]
 
-    lax.fori_loop(6, CHUNKS, input_chunk, 0)
+    lax.fori_loop(0, CHUNKS, input_chunk, 0)
     for i in range(1, 8):
         slot = xs.at[zr_[8 - i]]
         copy(slot, slot, sem_t_s.at[15 + i], sem_t_r.at[15 + i], mate).wait_recv()

time: 56.4 us -> 55.5 us (0.984)
  Pallas kernels: 55 us -> 54.1 us
    pallas_call x1, Pallas kernels: 52.9 us -> 52.1 us  [on_device(): pl.pallas_call(fused, out_shape=shapes, in_specs=[hbm] * 6, out_specs=[hb...]
where the time goes in v4:
time: 55.5 us; the launch traced here: 55.4 us
  Pallas kernels  54.1 us (97%)
  between operations  1.29 us (2%)
    pallas_call x1, Pallas kernels, on_device(): pl.pallas_call(fused, out_shape=shapes, in_specs=[hbm] * 6, out_specs=[hb...  52.1 us
    pallas_call x1, Pallas kernels, on_device(): pl.pallas_call(deliver, out_shape=shapes[:4] + (jax.ShapeDtypeStruct((D,)...  2.04 us

profile of v4, /device:TPU:1, one launch (start us, length us, event | category | flops | bytes accessed | tf_op | source)
XLA Modules:
  0.0 55.4 jit_solution(1875615060385886104)
XLA Ops:
  1.3 52.1 %conv_module.1 = (bf16[128,1536]{1,0:T(8,128)(2,1)}, bf16[128,1536]{1,0:T(8,128)(2,1)}, f32[6,1536]{1,0:T(8,128)}, f32[31,1536]{1,0:T(8,128)}, f32[1,1536]{1,0:T(1,128)}) custom-call(bf16[128,1536]{1,0:T(8,128)(2,1)} %bitcast.4, s32[1]{0:T(128)S(6)} %copy.11.len_hbm, f32[31,1536]{1,0:T(8,128)} %kern_hbm.1, f32[1536]{0:T(1024)} %gain_hbm.1, ...), custom_call_target="tpu_custom_call" | custom-call | tf_op jit(solution)/shard_map/conv_module/pallas_call | solution.py:679
  53.4 2.0 %deliver.1 = (bf16[128,1536]{1,0:T(8,128)(2,1)}, bf16[128,1536]{1,0:T(8,128)(2,1)}, f32[6,1536]{1,0:T(8,128)}, f32[31,1536]{1,0:T(8,128)}, f32[1536]{0:T(1024)}) custom-call(bf16[128,1536]{1,0:T(8,128)(2,1)} %get-tuple-element.15.refs_0_, bf16[128,1536]{1,0:T(8,128)(2,1)} %get-tuple-element.16.refs_1_, f32[6,1536]{1,0:T(8,128)} %get-tuple-element.17.refs_2_, ...), custom_call_target="tpu_custom_call" | custom-call | tf_op jit(solution)/shard_map/deliver/pallas_call | solution.py:690

commit v5 on v4

--- a/solution.py
+++ b/solution.py
@@ -318,42 +318,10 @@
 
         lax.fori_loop(0, H // LANES, mask_upstream, 0)
 
-    theirs = (1 - zp) * 2 + c
-    for part in range(4):
-        z_swaps[part].wait_recv()
-        here = atm.at[pl.ds(part * 192, 192), frames_of(theirs)]
-        swaps.append(send(here, here, sem_a_s.at[6 + part], sem_a_r.at[6 + part], mate))
-
-    told(2)
-
-    for item in swaps:
-        item.wait_recv()
-
-    def partial(n, start, width):
-        rows = pl.ds(pl.multiple_of(n * 192, 192), 192)
-        value = jnp.dot(atm[rows, :], ub[:, start:start + width], preferred_element_type=F32)
-        return value.reshape(4, 48, width).astype(BF16)
-
-    y_first = []
-    for i in (2, 1, 3, 0):
-        to_y = ys[i]
-        py[to_y] = partial(to_y, CX, CY)
-        if i:
-            y_first.append(send(py.at[to_y], ry.at[i - 1], sem_p_s.at[2 + i], sem_p_r.at[2 + i], along_y(i)))
-
-    def partial_x(n, _):
-        px[n] = partial(n, 0, CX)
-        return 0
-
-    lax.fori_loop(0, 4, partial_x, 0)
-    x_first = [
-        send(px.at[:, blocks[i]], rx.at[i - 1], sem_p_s.at[i - 1], sem_p_r.at[i - 1], along_x(i))
-        for i in (2, 1, 3)
-    ]
-
+    chip_rows = pl.ds(pl.multiple_of(zp * 2 * T, 2 * T), 2 * T)
     ag_swaps = []
-    chip_rows = pl.ds(pl.multiple_of(zp * 2 * T, 2 * T), 2 * T)
-    for n, from_y in ((6, y), (8, y_down), (10, y_up), (12, y_far)):
+
+    def act_grad(n, from_y):
         for side in range(2):
             landed(rows_of(from_y, 1 - xl, side), n + side)
         cols = pl.ds(pl.multiple_of(from_y * 384, 384), 384)
@@ -366,6 +334,45 @@
         ag_swaps.append(
             send(agp.at[oc, :, cols], agr.at[:, cols], sem_c_s.at[6 + k], sem_c_r.at[6 + k], mate)
         )
+
+    act_grad(6, y)
+
+    theirs = (1 - zp) * 2 + c
+    for part in range(4):
+        z_swaps[part].wait_recv()
+        here = atm.at[pl.ds(part * 192, 192), frames_of(theirs)]
+        swaps.append(send(here, here, sem_a_s.at[6 + part], sem_a_r.at[6 + part], mate))
+
+    told(2)
+
+    for item in swaps:
+        item.wait_recv()
+
+    def partial(n, start, width):
+        rows = pl.ds(pl.multiple_of(n * 192, 192), 192)
+        value = jnp.dot(atm[rows, :], ub[:, start:start + width], preferred_element_type=F32)
+        return value.reshape(4, 48, width).astype(BF16)
+
+    y_first = []
+    for i in (2, 1, 3, 0):
+        to_y = ys[i]
+        py[to_y] = partial(to_y, CX, CY)
+        if i:
+            y_first.append(send(py.at[to_y], ry.at[i - 1], sem_p_s.at[2 + i], sem_p_r.at[2 + i], along_y(i)))
+
+    def partial_x(n, _):
+        px[n] = partial(n, 0, CX)
+        return 0
+
+    lax.fori_loop(0, 4, partial_x, 0)
+    x_first = [
+        send(px.at[:, blocks[i]], rx.at[i - 1], sem_p_s.at[i - 1], sem_p_r.at[i - 1], along_x(i))
+        for i in (2, 1, 3)
+    ]
+
+    act_grad(8, y_down)
+    act_grad(10, y_up)
+    act_grad(12, y_far)
 
     for item in a_swaps:
         item.wait_recv()

time: 55.5 us -> 55 us (level)
  no operation moved by 1% of the time
where the time goes in v5:
time: 55 us; the launch traced here: 54.9 us
  Pallas kernels  53.6 us (97%)
  between operations  1.29 us (2%)
    pallas_call x1, Pallas kernels, on_device(): pl.pallas_call(fused, out_shape=shapes, in_specs=[hbm] * 6, out_specs=[hb...  51.6 us
    pallas_call x1, Pallas kernels, on_device(): pl.pallas_call(deliver, out_shape=shapes[:4] + (jax.ShapeDtypeStruct((D,)...  2.04 us

profile of v5, /device:TPU:1, one launch (start us, length us, event | category | flops | bytes accessed | tf_op | source)
XLA Modules:
  0.0 54.9 jit_solution(16799041138928564916)
XLA Ops:
  1.3 51.6 %conv_module.1 = (bf16[128,1536]{1,0:T(8,128)(2,1)}, bf16[128,1536]{1,0:T(8,128)(2,1)}, f32[6,1536]{1,0:T(8,128)}, f32[31,1536]{1,0:T(8,128)}, f32[1,1536]{1,0:T(1,128)}) custom-call(bf16[128,1536]{1,0:T(8,128)(2,1)} %bitcast.4, s32[1]{0:T(128)S(6)} %copy.11.len_hbm, f32[31,1536]{1,0:T(8,128)} %kern_hbm.1, f32[1536]{0:T(1024)} %gain_hbm.1, ...), custom_call_target="tpu_custom_call" | custom-call | tf_op jit(solution)/shard_map/conv_module/pallas_call | solution.py:686
  52.9 2.0 %deliver.1 = (bf16[128,1536]{1,0:T(8,128)(2,1)}, bf16[128,1536]{1,0:T(8,128)(2,1)}, f32[6,1536]{1,0:T(8,128)}, f32[31,1536]{1,0:T(8,128)}, f32[1536]{0:T(1024)}) custom-call(bf16[128,1536]{1,0:T(8,128)(2,1)} %get-tuple-element.15.refs_0_, bf16[128,1536]{1,0:T(8,128)(2,1)} %get-tuple-element.16.refs_1_, f32[6,1536]{1,0:T(8,128)} %get-tuple-element.17.refs_2_, ...), custom_call_target="tpu_custom_call" | custom-call | tf_op jit(solution)/shard_map/deliver/pallas_call | solution.py:697

commit v6 on v5

--- a/solution.py
+++ b/solution.py
@@ -585,10 +585,10 @@
     put_taps(half(c), fg)
     all_sent(late)
     gw_ref[:, half(c)] = fin[c][0:6]
+    w_swap.wait_recv()
+    gw_ref[:, half(oc)] = cr[0:6, :]
     t_swap.wait_recv()
     put_taps(half(oc), fgr)
-    w_swap.wait_recv()
-    gw_ref[:, half(oc)] = cr[0:6, :]
     for n, (src, dst) in enumerate(((gw_ref, gw_hbm), (gk_ref, gk_hbm), (gg_ref, gg_hbm))):
         stores.append(pltpu.make_async_copy(src, dst, sem_out.at[2 + n]))
         stores[-1].start()

time: 55 us -> 55 us (level)
  no operation moved by 1% of the time
where the time goes in v6:
time: 55 us; the launch traced here: 54.9 us
  Pallas kernels  53.6 us (97%)
  between operations  1.29 us (2%)
    pallas_call x1, Pallas kernels, on_device(): pl.pallas_call(fused, out_shape=shapes, in_specs=[hbm] * 6, out_specs=[hb...  51.5 us
    pallas_call x1, Pallas kernels, on_device(): pl.pallas_call(deliver, out_shape=shapes[:4] + (jax.ShapeDtypeStruct((D,)...  2.04 us

profile of v6, /device:TPU:1, one launch (start us, length us, event | category | flops | bytes accessed | tf_op | source)
XLA Modules:
  0.0 54.9 jit_solution(4126995714369925286)
XLA Ops:
  1.3 51.5 %conv_module.1 = (bf16[128,1536]{1,0:T(8,128)(2,1)}, bf16[128,1536]{1,0:T(8,128)(2,1)}, f32[6,1536]{1,0:T(8,128)}, f32[31,1536]{1,0:T(8,128)}, f32[1,1536]{1,0:T(1,128)}) custom-call(bf16[128,1536]{1,0:T(8,128)(2,1)} %bitcast.4, s32[1]{0:T(128)S(6)} %copy.11.len_hbm, f32[31,1536]{1,0:T(8,128)} %kern_hbm.1, f32[1536]{0:T(1024)} %gain_hbm.1, ...), custom_call_target="tpu_custom_call" | custom-call | tf_op jit(solution)/shard_map/conv_module/pallas_call | solution.py:686
  52.8 2.0 %deliver.1 = (bf16[128,1536]{1,0:T(8,128)(2,1)}, bf16[128,1536]{1,0:T(8,128)(2,1)}, f32[6,1536]{1,0:T(8,128)}, f32[31,1536]{1,0:T(8,128)}, f32[1536]{0:T(1024)}) custom-call(bf16[128,1536]{1,0:T(8,128)(2,1)} %get-tuple-element.15.refs_0_, bf16[128,1536]{1,0:T(8,128)(2,1)} %get-tuple-element.16.refs_1_, f32[6,1536]{1,0:T(8,128)} %get-tuple-element.17.refs_2_, ...), custom_call_target="tpu_custom_call" | custom-call | tf_op jit(solution)/shard_map/deliver/pallas_call | solution.py:697

commit v7 on v6

--- a/solution.py
+++ b/solution.py
@@ -360,6 +360,10 @@
         if i:
             y_first.append(send(py.at[to_y], ry.at[i - 1], sem_p_s.at[2 + i], sem_p_r.at[2 + i], along_y(i)))
 
+    act_grad(8, y_down)
+    act_grad(10, y_up)
+    act_grad(12, y_far)
+
     def partial_x(n, _):
         px[n] = partial(n, 0, CX)
         return 0
@@ -369,10 +373,6 @@
         send(px.at[:, blocks[i]], rx.at[i - 1], sem_p_s.at[i - 1], sem_p_r.at[i - 1], along_x(i))
         for i in (2, 1, 3)
     ]
-
-    act_grad(8, y_down)
-    act_grad(10, y_up)
-    act_grad(12, y_far)
 
     for item in a_swaps:
         item.wait_recv()

time: 55 us -> 55 us (level)
  no operation moved by 1% of the time
where the time goes in v7:
time: 55 us; the launch traced here: 54.9 us
  Pallas kernels  53.6 us (97%)
  between operations  1.29 us (2%)
    pallas_call x1, Pallas kernels, on_device(): pl.pallas_call(fused, out_shape=shapes, in_specs=[hbm] * 6, out_specs=[hb...  51.5 us
    pallas_call x1, Pallas kernels, on_device(): pl.pallas_call(deliver, out_shape=shapes[:4] + (jax.ShapeDtypeStruct((D,)...  2.04 us

profile of v7, /device:TPU:1, one launch (start us, length us, event | category | flops | bytes accessed | tf_op | source)
XLA Modules:
  0.0 54.9 jit_solution(8012270648868118204)
XLA Ops:
  1.3 51.5 %conv_module.1 = (bf16[128,1536]{1,0:T(8,128)(2,1)}, bf16[128,1536]{1,0:T(8,128)(2,1)}, f32[6,1536]{1,0:T(8,128)}, f32[31,1536]{1,0:T(8,128)}, f32[1,1536]{1,0:T(1,128)}) custom-call(bf16[128,1536]{1,0:T(8,128)(2,1)} %bitcast.4, s32[1]{0:T(128)S(6)} %copy.11.len_hbm, f32[31,1536]{1,0:T(8,128)} %kern_hbm.1, f32[1536]{0:T(1024)} %gain_hbm.1, ...), custom_call_target="tpu_custom_call" | custom-call | tf_op jit(solution)/shard_map/conv_module/pallas_call | solution.py:686
  52.8 2.0 %deliver.1 = (bf16[128,1536]{1,0:T(8,128)(2,1)}, bf16[128,1536]{1,0:T(8,128)(2,1)}, f32[6,1536]{1,0:T(8,128)}, f32[31,1536]{1,0:T(8,128)}, f32[1536]{0:T(1024)}) custom-call(bf16[128,1536]{1,0:T(8,128)(2,1)} %get-tuple-element.15.refs_0_, bf16[128,1536]{1,0:T(8,128)(2,1)} %get-tuple-element.16.refs_1_, f32[6,1536]{1,0:T(8,128)} %get-tuple-element.17.refs_2_, ...), custom_call_target="tpu_custom_call" | custom-call | tf_op jit(solution)/shard_map/deliver/pallas_call | solution.py:697
